TPU v7x, 128 devices: a whole 4x4x4 slice. The times are simulated.
128 devices in a mesh: tgt: 16 (over y_hi, z, core), sup: 8 (over y_lo, x).
Axes of the slice: x: 4, y: 4 (y_hi: 2, y_lo: 2; y = y_hi * 2 + y_lo), z: 4, core: 2. Of those that a mesh axis runs over, the one named last changes fastest.
Arguments:
- target_pool: float32 [1024, 3, 1024], P('tgt'), may hold values from -6 to 6
- target_index: int32 [128], P('tgt'), may hold values from 0 to 1023, as said below
- target_labels: int32 [128], P('tgt'), may hold values from 0 to 99
- dual_weights: float32 [512, 100], P('sup'), may hold values from -0.25 to 0.25
- support_images: float32 [512, 3, 1024], P(('sup', 'tgt')), may hold values from -6 to 6
Outputs:
- residual: float32 [128, 100], P('tgt')
- support_grad: float32 [512, 3, 1024], P(('sup', 'tgt'))
Inputs may be any that keep to these rules, and one draw needn't show every extreme that they name: `target_index`: for each j, the targets 8 * j to 8 * (j + 1) - 1 name distinct candidates among 64 * j to 64 * (j + 1) - 1.
All inputs are finite; a program needn't handle non-finite values.
Results may differ from a plain program's by a relative error of at most 0.0003.
Values sent between devices are 32-bit elements; how exact they have to be, the bound alone decides.
No kernel may reach another device: no remote copies, remote signals or barrier semaphores. Data moves between devices by JAX's collectives and lax.ppermute only.
A program may use at most 64 MiB of HBM per device.

v0:
```python
import math

import jax
import jax.numpy as jnp
import numpy as np
from jax import lax
from jax.experimental import pallas as pl
from jax.experimental.pallas import tpu as pltpu
from jax.sharding import PartitionSpec as P

SIDE = 32
CLASSES = 100
PIXELS = 1024
BETA = 0.01
TG = 32
SG = 8
ROWS = 8
DEEP = 16
AXES = ("tgt", "sup")
DIMS = (2, 4, 2, 2, 4)

TOP = (2.4493771255467647, 0.1932864690474489, -0.013754684085600787)
BOTTOM = (2.431483473487932, 3.4797192205950016)

VMEM = pl.BlockSpec(memory_space=pltpu.VMEM)
SMEM = pl.BlockSpec(memory_space=pltpu.SMEM)
F32 = jnp.float32


def pairs_of(move):
    out = []
    for src in range(int(np.prod(DIMS))):
        at = [int(v) for v in np.unravel_index(src, DIMS)]
        out.append((src, int(np.ravel_multi_index(move(*at), DIMS))))
    return out


def send(x, move):
    return lax.ppermute(x, AXES, pairs_of(move))


def even(v):
    return v ^ 1


def odd(v):
    return 3 - v


STEPS = (
    lambda yh, z, c, yl, x: (yh, even(z), c, yl, x),
    lambda yh, z, c, yl, x: (yh, odd(z), c, yl, x),
    lambda yh, z, c, yl, x: (yh, z, c, 1 - yl, x),
    lambda yh, z, c, yl, x: (yh, z, c, yl, even(x)),
    lambda yh, z, c, yl, x: (yh, z, c, yl, odd(x)),
)


def far_z(yh, z, c, yl, x):
    return (yh, z ^ 2, c, yl, x)


OTHERS = (
    lambda yh, z, c, yl, x: (yh, z, 1 - c, yl, x),
    lambda yh, z, c, yl, x: (1 - yh, z, c, yl, x),
    lambda yh, z, c, yl, x: (1 - yh, z, 1 - c, yl, x),
)


def rows_sum(v):
    lane = lax.broadcasted_iota(jnp.int32, v.shape[1:], 1)
    above = jnp.where(lane >= TG, pltpu.roll(v[ROWS - 1], TG, 1), 0.0)
    below = jnp.where(lane < 128 - TG, pltpu.roll(v[0], 128 - TG, 1), 0.0)
    up = jnp.concatenate([above[None], v[:-1]], axis=0)
    dn = jnp.concatenate([v[1:], below[None]], axis=0)
    return v + up + dn


def down(v):
    return jnp.concatenate([rows_sum(v[:ROWS]), rows_sum(v[ROWS:])], axis=0)


def target_box(v):
    col = lax.broadcasted_iota(jnp.int32, v.shape, 1)
    v = v + jnp.where(col == 0, 0.0, pltpu.roll(v, 1, 1)) + jnp.where(col == SIDE - 1, 0.0, pltpu.roll(v, SIDE - 1, 1))
    return rows_sum(v)


def triple(ref, j):
    return ref[pl.ds(j, 1)][0] + ref[pl.ds(j + 1, 1)][0] + ref[pl.ds(j + 2, 1)][0]


def wide(ref, k, j):
    one = jnp.broadcast_to(ref[k, :, pl.ds(j, 1), :], (ROWS, SG, 128))
    return jnp.concatenate([one, one], axis=0)


def pixel_box(v):
    lane = lax.broadcasted_iota(jnp.int32, v.shape, 1)
    col = lane & (SIDE - 1)
    v = v + jnp.where(col == 0, 0.0, pltpu.roll(v, 1, 1)) + jnp.where(col == SIDE - 1, 0.0, pltpu.roll(v, PIXELS - 1, 1))
    above = jnp.where(lane < SIDE, 0.0, pltpu.roll(v, SIDE, 1))
    below = jnp.where(lane >= PIXELS - SIDE, 0.0, pltpu.roll(v, PIXELS - SIDE, 1))
    return v + above + below


def spread_kernel(s_ref, y_ref, rb_ref, sb_ref, q_ref):
    def keep(k, v):
        for i in range(ROWS):
            row = jnp.concatenate([v[:, q * 256 + i * SIDE : q * 256 + (i + 1) * SIDE] for q in range(4)], axis=1)
            for g in range(2):
                q_ref[k, (g * ROWS + i) * SG : (g * ROWS + i + 1) * SG] = row[g * SG : (g + 1) * SG]

    energy = None
    for c in range(3):
        image = s_ref[c]
        energy = image * image if energy is None else energy + image * image
        keep(c, image * (1.0 / 27.0))
    level = pixel_box(energy * (1.0 / 27.0)) + BETA
    for l in range(3):
        inverse = lax.rsqrt(level)
        keep(3 + l, inverse)
        keep(6 + l, level * inverse * (1.0 / 9.0))
        if l < 2:
            level = pixel_box(level * (1.0 / 9.0)) + BETA

    first = lax.broadcasted_iota(jnp.int32, (DEEP * SG, 128), 1) // TG * SIDE

    def body(j, carry):
        for k in range(9):
            ref = (y_ref, rb_ref, sb_ref)[k // 3]
            one = jnp.take_along_axis(q_ref[k], first + j, axis=1)
            ref[k % 3, pl.ds(j, 1)] = one.reshape(1, DEEP, SG, 128)
        return carry

    lax.fori_loop(0, SIDE, body, 0, unroll=2)


def spread(ref, k, j):
    return ref[k, pl.ds(j, 1)][0]


def forward_kernel(
    place_ref, x_ref, y_ref, rb_ref, sb_ref, dual_ref,
    pred_ref, xt_ref, h0_ref, h1_ref, w0_ref, w1_ref, w2_ref, v2_ref,
    ra_ref, sa_ref, va_ref, vb_ref,
):
    energy = None
    for c in range(3):
        parts = []
        for q in range(4):
            for r in range(4):
                parts.append(x_ref[r, c * 8 : (c + 1) * 8, q * 256 : (q + 1) * 256])
        turned = jnp.concatenate(parts, axis=0).T.reshape(ROWS, SIDE, 128)
        xt_ref[c] = turned
        energy = turned * turned if energy is None else energy + turned * turned
    level = target_box(energy * (1.0 / 27.0)) + BETA
    for l in range(3):
        inverse = lax.rsqrt(level)
        ra_ref[l] = inverse
        sa_ref[l] = level * inverse * (1.0 / math.pi)
        if l < 2:
            level = target_box(level * (1.0 / 9.0)) + BETA

    clear_edges(va_ref, vb_ref, v2_ref)

    def inner(j, carry):
        total = spread(y_ref, 0, j) * wide(xt_ref, 0, j)
        total = total + spread(y_ref, 1, j) * wide(xt_ref, 1, j)
        total = total + spread(y_ref, 2, j) * wide(xt_ref, 2, j)
        va_ref[pl.ds(j + 1, 1)] = down(total)[None]
        return carry

    lax.fori_loop(0, SIDE, inner, 0, unroll=2)

    def layer(l, j, from_ref):
        cross = triple(from_ref, j) + BETA
        x = cross * (spread(rb_ref, l, j) * wide(ra_ref, l, j))
        u = jnp.abs(x) if l == 0 else x
        d = jnp.maximum(1.0 - u * u, 1e-30)
        s = d * lax.rsqrt(d)
        top = (u * (TOP[2] / (9.0 * math.pi)) + TOP[1] / (9.0 * math.pi)) * u + TOP[0] / (9.0 * math.pi)
        q = s * (top * lax.rsqrt((u + BOTTOM[1]) * u + BOTTOM[0]))
        h = 1.0 / 9.0 - q
        if l == 0:
            h = jnp.where(x >= 0.0, h, q)
        w = (spread(sb_ref, l, j) * wide(sa_ref, l, j)) * s
        return h, w, w + h * cross

    def layer0(j, carry):
        h, w, f = layer(0, j, va_ref)
        h0_ref[pl.ds(j, 1)] = h[None]
        w0_ref[pl.ds(j, 1)] = w[None]
        vb_ref[pl.ds(j + 1, 1)] = down(f)[None]
        return carry

    def layer1(j, carry):
        h, w, f = layer(1, j, vb_ref)
        h1_ref[pl.ds(j, 1)] = h[None]
        w1_ref[pl.ds(j, 1)] = w[None]
        va_ref[pl.ds(j + 1, 1)] = down(f)[None]
        return carry

    def layer2(j, total):
        h, w, f = layer(2, j, va_ref)
        w2_ref[pl.ds(j, 1)] = w[None]
        v2_ref[pl.ds(j + 1, 1)] = down(h)[None]
        return total + jnp.sum(f.reshape(2, ROWS, SG, 128), axis=1)

    lax.fori_loop(0, SIDE, layer0, 0, unroll=4)
    lax.fori_loop(0, SIDE, layer1, 0, unroll=4)
    total = lax.fori_loop(0, SIDE, layer2, jnp.zeros((2, SG, 128), F32), unroll=4)
    kernel = total * (9.0 / PIXELS)
    wide_pred = None
    for g in range(2):
        part = lax.dot_general(
            kernel[g], dual_ref[g * SG : (g + 1) * SG], (((0,), (0,)), ((), ())),
            precision=lax.Precision.HIGHEST, preferred_element_type=F32,
        )
        wide_pred = part if wide_pred is None else wide_pred + part
    pred = wide_pred[:32] + wide_pred[32:64] + wide_pred[64:96] + wide_pred[96:]
    for r in range(4):
        pred_ref[pl.ds(pl.multiple_of(place_ref[r] * 8, 8), 8), :] = pred[r * 8 : (r + 1) * 8]


def clear_edges(*refs):
    for ref in refs:
        ref[0] = jnp.zeros((DEEP, SG, 128), F32)
        ref[SIDE + 1] = jnp.zeros((DEEP, SG, 128), F32)


def at(ref, j):
    return ref[pl.ds(j, 1)][0]


def back_kernel_a(v2_ref, h1_ref, w1_ref, w2_ref, rb_ref, l1_ref, v1_ref, p2_ref):
    clear_edges(v1_ref, p2_ref)

    def body(j, carry):
        up = triple(v2_ref, j)
        rb = spread(rb_ref, 1, j)
        l1_ref[pl.ds(j, 1)] = (up * at(w1_ref, j) * (rb * rb))[None]
        v1_ref[pl.ds(j + 1, 1)] = down(up * at(h1_ref, j))[None]
        rb = spread(rb_ref, 2, j)
        p2_ref[pl.ds(j + 1, 1)] = down(at(w2_ref, j) * (rb * rb))[None]
        return carry

    lax.fori_loop(0, SIDE, body, 0, unroll=4)


def back_kernel_b(v1_ref, h0_ref, w0_ref, l1_ref, p2_ref, rb_ref, l0_ref, v0_ref, p1_ref):
    clear_edges(v0_ref, p1_ref)

    def body(j, carry):
        up = triple(v1_ref, j)
        rb = spread(rb_ref, 0, j)
        l0_ref[pl.ds(j, 1)] = (up * at(w0_ref, j) * (rb * rb))[None]
        v0_ref[pl.ds(j + 1, 1)] = down(up * at(h0_ref, j))[None]
        p1_ref[pl.ds(j + 1, 1)] = down(at(l1_ref, j) + triple(p2_ref, j) * (1.0 / 9.0))[None]
        return carry

    lax.fori_loop(0, SIDE, body, 0, unroll=4)


def back_kernel_c(l0_ref, p1_ref, p0_ref):
    clear_edges(p0_ref)

    def body(j, carry):
        p0_ref[pl.ds(j + 1, 1)] = down(at(l0_ref, j) + triple(p1_ref, j) * (1.0 / 9.0))[None]
        return carry

    lax.fori_loop(0, SIDE, body, 0, unroll=4)


def back_kernel_d(v0_ref, p0_ref, up_ref, energy_ref):
    def body(j, carry):
        up_ref[pl.ds(j, 1)] = triple(v0_ref, j)[None]
        energy_ref[pl.ds(j, 1)] = (triple(p0_ref, j) * 27.0)[None]
        return carry

    lax.fori_loop(0, SIDE, body, 0, unroll=4)


def back_kernel_e(up_ref, energy_ref, xt_ref, y_ref, g_ref):
    def body(j, carry):
        up, energy = at(up_ref, j), at(energy_ref, j)
        for c in range(3):
            g_ref[c, pl.ds(j, 1)] = (up * wide(xt_ref, c, j) + energy * spread(y_ref, c, j))[None]
        return carry

    lax.fori_loop(0, SIDE, body, 0, unroll=2)


def fold(a, b, step):
    lane = lax.broadcasted_iota(jnp.int32, a.shape, 1)
    return jnp.where((lane & step) == 0, a + pltpu.roll(a, 128 - step, 1), b + pltpu.roll(b, step, 1))


def sum_kernel(place_ref, res_ref, dual_ref, g_ref, own_ref, *out_refs):
    own_ref[...] = res_ref[pl.ds(pl.multiple_of(place_ref[0] * 8, 8), 8), :]
    rows = [res_ref[pl.ds(pl.multiple_of(place_ref[r] * 8, 8), 8), :] for r in range(4)]
    weight = lax.dot_general(
        dual_ref[...] * (1.0 / 3.0), jnp.concatenate(rows * 4, axis=0), (((1,), (1,)), ((), ())),
        precision=lax.Precision.HIGHEST, preferred_element_type=F32,
    )
    weight = jnp.broadcast_to(weight.reshape(2, 1, SG, 128), (2, ROWS, SG, 128)).reshape(DEEP, SG, 128)
    row = lax.broadcasted_iota(jnp.int32, (512, 128), 0)
    col = lax.broadcasted_iota(jnp.int32, (512, 128), 1)
    place = col - (row & 127) // TG * SIDE - (row & 31) // 8 - lax.shift_right_logical(row, 7) * 4
    total = jnp.zeros((3 * 128, 128), F32)
    for j in range(0, SIDE, 16):
        pick = jnp.where(place == j, 1.0, 0.0).astype(jnp.bfloat16)
        his, lows = [], []
        for k in range(j, j + 16, 4):
            four = [(g_ref[:, k + n] * weight).reshape(3 * 128, 128) for n in range(4)]
            term = fold(fold(four[0], four[2], 16), fold(four[1], four[3], 16), 8)
            hi = term.astype(jnp.bfloat16)
            his.append(hi)
            lows.append((term - hi.astype(F32)).astype(jnp.bfloat16))
        total = total + jnp.dot(jnp.concatenate(his, axis=1), pick, preferred_element_type=F32)
        total = total + jnp.dot(jnp.concatenate(lows, axis=1), pick, preferred_element_type=F32)
    for c in range(3):
        for g in range(2):
            image = [total[((c * 2 + g) * ROWS + i) * SG : ((c * 2 + g) * ROWS + i + 1) * SG] for i in range(ROWS)]
            line = jnp.concatenate([image[i][:, q * SIDE : (q + 1) * SIDE] for q in range(4) for i in range(ROWS)], axis=1)
            out_refs[2 * g][c] = line[:4]
            out_refs[2 * g + 1][c] = line[4:]


def near(x):
    return pltpu.with_memory_space_constraint(x, pltpu.VMEM)


def vm(*shape):
    return pltpu.VMEM(shape, F32)


def hb(*shape):
    return jax.ShapeDtypeStruct(shape, F32)


def params(mib):
    return pltpu.CompilerParams(vmem_limit_bytes=mib << 20)


def shards(target_pool, target_index, target_labels, dual_weights, support_images):
    tgt = lax.axis_index("tgt")
    sup = lax.axis_index("sup")
    z = (tgt // 2) % 4

    mine = support_images.transpose(1, 0, 2)
    near_images = send(mine, OTHERS[0])
    others = [near_images, send(mine, OTHERS[1]), send(mine, OTHERS[2])]
    target_index, near_images = lax.optimization_barrier((target_index, near_images))
    support = jnp.concatenate([mine] + others, axis=1)
    targets = target_pool.at[target_index - tgt * target_pool.shape[0]].get(mode="promise_in_bounds")
    block = targets.transpose(1, 0, 2).reshape(24, PIXELS)
    x_all = jnp.stack([block, send(block, STEPS[0]), send(block, STEPS[1]), send(block, far_z)])
    place = jnp.stack([z, z ^ 1, 3 - z, z ^ 2]).astype(jnp.int32)

    duals = jnp.concatenate(
        [lax.dynamic_slice_in_dim(dual_weights, (tgt ^ k) * 4, 4, 0) for k in (0, 1, 8, 9)]
    )
    spread_shape = (3, SIDE, DEEP, SG, 128)
    y_wide, rb_wide, sb_wide = pl.pallas_call(
        spread_kernel, out_shape=(vm(*spread_shape),) * 3, in_specs=[VMEM], out_specs=(VMEM,) * 3,
        scratch_shapes=[pltpu.VMEM((9, DEEP * SG, 128), F32)], compiler_params=params(6), name="spread",
    )(support)

    column = (SIDE, DEEP, SG, 128)
    padded = (SIDE + 2, DEEP, SG, 128)
    flat = (3, ROWS, SIDE, 128)

    def near_call(kernel, outs, ins, name, scratch=(), mib=6):
        return pl.pallas_call(
            kernel, out_shape=tuple(vm(*o) for o in outs), in_specs=[VMEM] * len(ins), out_specs=(VMEM,) * len(outs),
            scratch_shapes=[pltpu.VMEM(v, F32) for v in scratch], compiler_params=params(mib), name=name,
        )(*map(near, ins))

    pred, xt, h0, h1, w0, w1, w2, v2 = pl.pallas_call(
        forward_kernel,
        out_shape=(hb(TG, CLASSES), vm(*flat), vm(*column), vm(*column), vm(*column), vm(*column), vm(*column), vm(*padded)),
        in_specs=[SMEM] + [VMEM] * 5,
        out_specs=(VMEM,) * 8,
        scratch_shapes=[pltpu.VMEM(flat, F32), pltpu.VMEM(flat, F32), pltpu.VMEM(padded, F32), pltpu.VMEM(padded, F32)],
        compiler_params=params(14), name="forward",
    )(place, x_all, near(y_wide), near(rb_wide), near(sb_wide), duals)

    labels = jnp.tile(target_labels, 4)
    hot = ((jnp.arange(TG) // 8 == z) & (sup == 0))[:, None] & (labels[:, None] == jnp.arange(CLASSES)[None, :])
    res = pred - hot.astype(F32)

    res, v2 = lax.optimization_barrier((res, v2))
    new = send(res, STEPS[0])
    l1, v1, p2 = near_call(back_kernel_a, (column, padded, padded), (v2, h1, w1, w2, rb_wide), "back_a")
    res, v1 = lax.optimization_barrier((res + new, v1))
    new = send(res, STEPS[1])
    l0, v0, p1 = near_call(back_kernel_b, (column, padded, padded), (v1, h0, w0, l1, p2, rb_wide), "back_b")
    res, l0 = lax.optimization_barrier((res + new, l0))
    new = send(res, STEPS[2])
    (p0,) = near_call(back_kernel_c, (padded,), (l0, p1), "back_c")
    res, p0 = lax.optimization_barrier((res + new, p0))
    new = send(res, STEPS[3])
    up, energy = near_call(back_kernel_d, (column, column), (v0, p0), "back_d")
    res, up = lax.optimization_barrier((res + new, up))
    new = send(res, STEPS[4])
    (g,) = near_call(back_kernel_e, ((3,) + column,), (up, energy, xt, y_wide), "back_e")
    res = res + new

    residual, *parts = pl.pallas_call(
        sum_kernel, out_shape=(hb(8, CLASSES),) + (hb(3, 4, PIXELS),) * 4,
        in_specs=[SMEM] + [VMEM] * 3, out_specs=(VMEM,) * 5,
        compiler_params=params(10), name="weighted",
    )(place, res, duals, near(g))
    far1, far2 = send(parts[2], OTHERS[1]), send(parts[3], OTHERS[2])
    total = parts[0] + send(parts[1], OTHERS[0]) + far1 + far2
    return (residual, total.transpose(1, 0, 2))


def solution(mesh):
    in_specs = (
        P("tgt", None, None),
        P("tgt"),
        P("tgt"),
        P("sup", None),
        P(("sup", "tgt"), None, None),
    )
    out_specs = (P("tgt", None), P(("sup", "tgt"), None, None))
    return jax.shard_map(shards, mesh=mesh, in_specs=in_specs, out_specs=out_specs, check_vma=False)
```

profile of v0, /device:TPU:0, one launch (start us, length us, event | category | flops | bytes accessed | tf_op | source)
XLA Modules:
  0.0 64.4 jit_solution(2687805557716535679)
XLA Ops:
  0.6 2.8 %collective-permute-start.5 = (f32[3,4,1024]{2,1,0:T(4,128)}, f32[3,4,1024]{2,1,0:T(4,128)S(1)}, u32[]{:S(2)}, u32[]{:S(2)}) collective-permute-start(f32[3,4,1024]{2,1,0:T(4,128)} %bitcast.22), channel_id=1, source_target_pairs={{0,72},{1,73},{2,74},{3,75},{4,76},{5,77},{6,78},{7,79},{8,64},{9,... | collective-permute-start | bytes 147464 | tf_op jit(solution)/shard_map/ppermute | solution.py:39
  4.1 0.8 %constant_dynamic-slice_fusion.3 = (f32[4,100]{1,0:T(4,128)S(1)}, f32[4,100]{1,0:T(4,128)S(1)}, f32[4,100]{1,0:T(4,128)S(1)}, f32[4,100]{1,0:T(4,128)S(1)}) fusion(f32[64,100]{1,0:T(8,128)} %param.8, s32[]{:T(128)S(6)} %select_n.38, s32[]{:T(128)S(6)} %select_n.39, s32[]{:T(128)S(6)} %select_n.41, s32[]{:T(128)S(6)} %select_n.40), kind=kLoop, calls=%fused_computation.18 | loop fusion | bytes 12816 | tf_op jit(solution)/shard_map/dynamic_slice | solution.py:362
  7.1 4.0 %collective-permute-start.3 = (f32[24,1024]{1,0:T(8,128)S(1)}, f32[24,1024]{1,0:T(8,128)S(1)}, u32[]{:S(2)}, u32[]{:S(2)}) collective-permute-start(f32[24,1024]{1,0:T(8,128)S(1)} %bitcast.15), channel_id=1, source_target_pairs={{0,32},{1,33},{2,34},{3,35},{4,36},{5,37},{6,38},{7,39},{8,40},{9,... | collective-permute-start | bytes 294920 | tf_op jit(solution)/shard_map/ppermute | solution.py:39
  12.1 0.8 %pad_maximum_fusion.1.s_ref = f32[3,16,1024]{2,1,0:T(8,128)S(1)} fusion(f32[3,4,1024]{2,1,0:T(4,128)S(1)} %collective-permute-done.5, f32[3,4,1024]{2,1,0:T(4,128)S(1)} %collective-permute-done.4, f32[3,4,1024]{2,1,0:T(4,128)S(1)} %collective-permute-done, f32[3,4,1024]{2,1,0:T(4,128)} %bitcast.25), kind=kLoop, calls=%fused_computation.2 | loop fusion | flops 147456 | bytes 393216 | tf_op jit(solution)/shard_map/concatenate | solution.py:355
  13.0 7.1 %spread.1 = (f32[3,32,16,8,128]{4,3,2,1,0:T(8,128)S(1)}, f32[3,32,16,8,128]{4,3,2,1,0:T(8,128)S(1)}, f32[3,32,16,8,128]{4,3,2,1,0:T(8,128)S(1)}) custom-call(f32[3,16,1024]{2,1,0:T(8,128)S(1)} %pad_maximum_fusion.1.s_ref), custom_call_target="tpu_custom_call" | custom-call | tf_op jit(solution)/shard_map/spread/pallas_call | solution.py:365
  20.2 9.4 %forward.1 = (f32[32,100]{1,0:T(8,128)S(1)}, f32[3,8,32,128]{3,2,1,0:T(8,128)S(1)}, f32[32,16,8,128]{3,2,1,0:T(8,128)S(1)}, f32[32,16,8,128]{3,2,1,0:T(8,128)S(1...) custom-call(s32[4]{0:T(128)S(1)} %pad_add_fusion.place_ref, ...), custom_call_target="tpu_custom_call" | custom-call | tf_op jit(solution)/shard_map/forward/pallas_call | solution.py:380
  29.7 1.8 %collective-permute-start.6 = (f32[32,100]{1,0:T(8,128)S(1)}, f32[32,100]{1,0:T(8,128)S(1)}, u32[]{:S(2)}, u32[]{:S(2)}) collective-permute-start(f32[32,100]{1,0:T(8,128)S(1)} %convert_subtract_fusion), channel_id=1, source_target_pairs={{0,16},{1,17},{2,18},{3,19},{4,20},{5,21},{6,22},{7,23},{8,24},{9,... | collective-permute-start | bytes 38408 | tf_op jit(solution)/shard_map/ppermute | solution.py:39
  31.5 1.1 %back_a.1 = (f32[32,16,8,128]{3,2,1,0:T(8,128)S(1)}, f32[34,16,8,128]{3,2,1,0:T(8,128)S(1)}, f32[34,16,8,128]{3,2,1,0:T(8,128)S(1)}) custom-call(f32[34,16,8,128]{3,2,1,0:T(8,128)S(1)} %get-tuple-element.44.v2_ref, f32[32,16,8,128]{3,2,1,0:T(8,128)S(1)} %get-tuple-element.45.h1_ref, f32[32,16,8,128]{3,2,1,0:T(8,128)S(1)} %get-tuple-element.46.w1_ref, ...), custom_call_target="tpu_custom_call" | custom-call | tf_op jit(solution)/shard_map/back_a/pallas_call | solution.py:375
  32.6 0.9 %collective-permute-done.6 = f32[32,100]{1,0:T(8,128)S(1)} collective-permute-done((f32[32,100]{1,0:T(8,128)S(1)}, f32[32,100]{1,0:T(8,128)S(1)}, u32[]{:S(2)}, u32[]{:S(2)}) %collective-permute-start.6) | collective-permute-done | bytes 12832 | tf_op jit(solution)/shard_map/ppermute | solution.py:39
  33.5 2.6 %collective-permute-start.7 = (f32[32,100]{1,0:T(8,128)S(1)}, f32[32,100]{1,0:T(8,128)S(1)}, u32[]{:S(2)}, u32[]{:S(2)}) collective-permute-start(f32[32,100]{1,0:T(8,128)S(1)} %add.55), channel_id=1, source_target_pairs={{0,48},{1,49},{2,50},{3,51},{4,52},{5,53},{6,54},{7,55},{8,56},{9,... | collective-permute-start | bytes 38408 | tf_op jit(solution)/shard_map/ppermute | solution.py:39
  36.1 1.4 %back_b.1 = (f32[32,16,8,128]{3,2,1,0:T(8,128)S(1)}, f32[34,16,8,128]{3,2,1,0:T(8,128)S(1)}, f32[34,16,8,128]{3,2,1,0:T(8,128)S(1)}) custom-call(f32[34,16,8,128]{3,2,1,0:T(8,128)S(1)} %get-tuple-element.50.v1_ref, f32[32,16,8,128]{3,2,1,0:T(8,128)S(1)} %get-tuple-element.51.h0_ref, f32[32,16,8,128]{3,2,1,0:T(8,128)S(1)} %get-tuple-element.52.w0_ref, ...), custom_call_target="tpu_custom_call" | custom-call | tf_op jit(solution)/shard_map/back_b/pallas_call | solution.py:375
  37.5 0.9 %collective-permute-done.7 = f32[32,100]{1,0:T(8,128)S(1)} collective-permute-done((f32[32,100]{1,0:T(8,128)S(1)}, f32[32,100]{1,0:T(8,128)S(1)}, u32[]{:S(2)}, u32[]{:S(2)}) %collective-permute-start.7) | collective-permute-done | bytes 12832 | tf_op jit(solution)/shard_map/ppermute | solution.py:39
  38.4 1.6 %collective-permute-start.8 = (f32[32,100]{1,0:T(8,128)S(1)}, f32[32,100]{1,0:T(8,128)S(1)}, u32[]{:S(2)}, u32[]{:S(2)}) collective-permute-start(f32[32,100]{1,0:T(8,128)S(1)} %add.56), channel_id=1, source_target_pairs={{0,4},{1,5},{2,6},{3,7},{4,0},{5,1},{6,2},{7,3},{8,12},{9,13},{10,... | collective-permute-start | bytes 38408 | tf_op jit(solution)/shard_map/ppermute | solution.py:39
  40.0 0.7 %back_c.1.p0_ref = f32[34,16,8,128]{3,2,1,0:T(8,128)S(1)} custom-call(f32[32,16,8,128]{3,2,1,0:T(8,128)S(1)} %get-tuple-element.57.l0_ref, f32[34,16,8,128]{3,2,1,0:T(8,128)S(1)} %get-tuple-element.58.p1_ref), custom_call_target="tpu_custom_call" | custom-call | tf_op jit(solution)/shard_map/back_c/pallas_call | solution.py:375
  40.8 1.4 %collective-permute-done.8 = f32[32,100]{1,0:T(8,128)S(1)} collective-permute-done((f32[32,100]{1,0:T(8,128)S(1)}, f32[32,100]{1,0:T(8,128)S(1)}, u32[]{:S(2)}, u32[]{:S(2)}) %collective-permute-start.8) | collective-permute-done | bytes 12832 | tf_op jit(solution)/shard_map/ppermute | solution.py:39
  42.2 1.5 %collective-permute-start.9 = (f32[32,100]{1,0:T(8,128)S(1)}, f32[32,100]{1,0:T(8,128)S(1)}, u32[]{:S(2)}, u32[]{:S(2)}) collective-permute-start(f32[32,100]{1,0:T(8,128)S(1)} %add.57), channel_id=1, source_target_pairs={{0,1},{1,0},{2,3},{3,2},{4,5},{5,4},{6,7},{7,6},{8,9},{9,8},{10,11... | collective-permute-start | bytes 38408 | tf_op jit(solution)/shard_map/ppermute | solution.py:39
  44.2 1.7 %collective-permute-done.9 = f32[32,100]{1,0:T(8,128)S(1)} collective-permute-done((f32[32,100]{1,0:T(8,128)S(1)}, f32[32,100]{1,0:T(8,128)S(1)}, u32[]{:S(2)}, u32[]{:S(2)}) %collective-permute-start.9) | collective-permute-done | bytes 12832 | tf_op jit(solution)/shard_map/ppermute | solution.py:39
  45.9 2.8 %collective-permute-start.10 = (f32[32,100]{1,0:T(8,128)S(1)}, f32[32,100]{1,0:T(8,128)S(1)}, u32[]{:S(2)}, u32[]{:S(2)}) collective-permute-start(f32[32,100]{1,0:T(8,128)S(1)} %add.58), channel_id=1, source_target_pairs={{0,3},{1,2},{2,1},{3,0},{4,7},{5,6},{6,5},{7,4},{8,11},{9,10},{10,... | collective-permute-start | bytes 38408 | tf_op jit(solution)/shard_map/ppermute | solution.py:39
  48.7 1.0 %back_e.1.g_ref = f32[3,32,16,8,128]{4,3,2,1,0:T(8,128)S(1)} custom-call(f32[32,16,8,128]{3,2,1,0:T(8,128)S(1)} %get-tuple-element.64.up_ref, f32[32,16,8,128]{3,2,1,0:T(8,128)S(1)} %get-tuple-element.65.energy_ref, f32[3,8,32,128]{3,2,1,0:T(8,128)S(1)} %get-tuple-element.66.xt_ref, f32[3,32,16,8,128]{4,3,2,1,0:T(8,128)S(1)} %get-tuple-element.38.y_ref), custom_call_target="tpu_custom_call" | custom-call | tf_op jit(solution)/shard_map/back_e/pallas_call | solution.py:375
  49.7 1.2 %collective-permute-done.10 = f32[32,100]{1,0:T(8,128)S(1)} collective-permute-done((f32[32,100]{1,0:T(8,128)S(1)}, f32[32,100]{1,0:T(8,128)S(1)}, u32[]{:S(2)}, u32[]{:S(2)}) %collective-permute-start.10) | collective-permute-done | bytes 12832 | tf_op jit(solution)/shard_map/ppermute | solution.py:39
  50.9 4.4 %weighted.1 = (f32[8,100]{1,0:T(8,128)}, f32[3,4,1024]{2,1,0:T(4,128)S(1)}, f32[3,4,1024]{2,1,0:T(4,128)S(1)}, f32[3,4,1024]{2,1,0:T(4,128)S(1)}, f32[3,4,1024]{2,1,0:T(4,128)S(1)}) custom-call(s32[4]{0:T(128)S(1)} %pad_add_fusion.place_ref, f32[32,100]{1,0:T(8,128)S(1)} %add.59.res_ref, f32[16,100]{1,0:T(8,128)S(1)} %pad_maximum_fusion.2.dual_ref, ...), custom_call_target="tpu_custom_call" | custom-call | tf_op jit(solution)/shard_map/weighted/pallas_call | solution.py:410
  55.3 3.2 %collective-permute-start.12 = (f32[3,4,1024]{2,1,0:T(4,128)S(1)}, f32[3,4,1024]{2,1,0:T(4,128)S(1)}, u32[]{:S(2)}, u32[]{:S(2)}) collective-permute-start(f32[3,4,1024]{2,1,0:T(4,128)S(1)} %get-tuple-element.70), channel_id=1, source_target_pairs={{0,64},{1,65},{2,66},{3,67},{4,68},{5,69},{6,70},{7,71},{8,72},{9,... | collective-permute-start | bytes 147464 | tf_op jit(solution)/shard_map/ppermute | solution.py:39
  58.7 2.3 %collective-permute-done.12 = f32[3,4,1024]{2,1,0:T(4,128)S(1)} collective-permute-done((f32[3,4,1024]{2,1,0:T(4,128)S(1)}, f32[3,4,1024]{2,1,0:T(4,128)S(1)}, u32[]{:S(2)}, u32[]{:S(2)}) %collective-permute-start.12) | collective-permute-done | bytes 49184 | tf_op jit(solution)/shard_map/ppermute | solution.py:39
  61.0 2.8 %collective-permute-done.13 = f32[3,4,1024]{2,1,0:T(4,128)S(1)} collective-permute-done((f32[3,4,1024]{2,1,0:T(4,128)S(1)}, f32[3,4,1024]{2,1,0:T(4,128)S(1)}, u32[]{:S(2)}, u32[]{:S(2)}) %collective-permute-start.13) | collective-permute-done | bytes 49184 | tf_op jit(solution)/shard_map/ppermute | solution.py:39
  (32 shorter events, 5.4 us)
Async XLA Ops:
  0.6 5.8 %copy-start = (f32[64,3,1024]{2,0,1:T(8,128)S(1)}, f32[64,3,1024]{2,0,1:T(8,128)}, u32[]{:S(2)}) copy-start(f32[64,3,1024]{2,0,1:T(8,128)} %param.5) | copy-start | bytes 2359300
  0.6 11.5 %collective-permute-start.5 = (f32[3,4,1024]{2,1,0:T(4,128)}, f32[3,4,1024]{2,1,0:T(4,128)S(1)}, u32[]{:S(2)}, u32[]{:S(2)}) collective-permute-start(f32[3,4,1024]{2,1,0:T(4,128)} %bitcast.22), channel_id=1, source_target_pairs={{0,72},{1,73},{2,74},{3,75},{4,76},{5,77},{6,78},{7,79},{8,64},{9,... | collective-permute-start | bytes 147464 | tf_op jit(solution)/shard_map/ppermute | solution.py:39
  3.4 8.7 %collective-permute-start.4 = (f32[3,4,1024]{2,1,0:T(4,128)}, f32[3,4,1024]{2,1,0:T(4,128)S(1)}, u32[]{:S(2)}, u32[]{:S(2)}) collective-permute-start(f32[3,4,1024]{2,1,0:T(4,128)} %bitcast.23), channel_id=1, source_target_pairs={{0,64},{1,65},{2,66},{3,67},{4,68},{5,69},{6,70},{7,71},{8,72},{9,... | collective-permute-start | bytes 147464 | tf_op jit(solution)/shard_map/ppermute | solution.py:39
  4.1 1.7 %collective-permute-start = (f32[3,4,1024]{2,1,0:T(4,128)}, f32[3,4,1024]{2,1,0:T(4,128)S(1)}, u32[]{:S(2)}, u32[]{:S(2)}) collective-permute-start(f32[3,4,1024]{2,1,0:T(4,128)} %bitcast.24), channel_id=1, source_target_pairs={{0,8},{1,9},{2,10},{3,11},{4,12},{5,13},{6,14},{7,15},{8,0},{9,1},... | collective-permute-start | bytes 147464 | tf_op jit(solution)/shard_map/ppermute | solution.py:39
  7.1 13.0 %collective-permute-start.3 = (f32[24,1024]{1,0:T(8,128)S(1)}, f32[24,1024]{1,0:T(8,128)S(1)}, u32[]{:S(2)}, u32[]{:S(2)}) collective-permute-start(f32[24,1024]{1,0:T(8,128)S(1)} %bitcast.15), channel_id=1, source_target_pairs={{0,32},{1,33},{2,34},{3,35},{4,36},{5,37},{6,38},{7,39},{8,40},{9,... | collective-permute-start | bytes 294920 | tf_op jit(solution)/shard_map/ppermute | solution.py:39
  11.1 9.0 %collective-permute-start.2 = (f32[24,1024]{1,0:T(8,128)S(1)}, f32[24,1024]{1,0:T(8,128)S(1)}, u32[]{:S(2)}, u32[]{:S(2)}) collective-permute-start(f32[24,1024]{1,0:T(8,128)S(1)} %bitcast.16), channel_id=1, source_target_pairs={{0,48},{1,49},{2,50},{3,51},{4,52},{5,53},{6,54},{7,55},{8,56},{9,... | collective-permute-start | bytes 294920 | tf_op jit(solution)/shard_map/ppermute | solution.py:39
  11.8 8.3 %collective-permute-start.1 = (f32[24,1024]{1,0:T(8,128)S(1)}, f32[24,1024]{1,0:T(8,128)S(1)}, u32[]{:S(2)}, u32[]{:S(2)}) collective-permute-start(f32[24,1024]{1,0:T(8,128)S(1)} %bitcast.17), channel_id=1, source_target_pairs={{0,16},{1,17},{2,18},{3,19},{4,20},{5,21},{6,22},{7,23},{8,24},{9,... | collective-permute-start | bytes 294920 | tf_op jit(solution)/shard_map/ppermute | solution.py:39
  29.7 3.8 %collective-permute-start.6 = (f32[32,100]{1,0:T(8,128)S(1)}, f32[32,100]{1,0:T(8,128)S(1)}, u32[]{:S(2)}, u32[]{:S(2)}) collective-permute-start(f32[32,100]{1,0:T(8,128)S(1)} %convert_subtract_fusion), channel_id=1, source_target_pairs={{0,16},{1,17},{2,18},{3,19},{4,20},{5,21},{6,22},{7,23},{8,24},{9,... | collective-permute-start | bytes 38408 | tf_op jit(solution)/shard_map/ppermute | solution.py:39
  33.5 4.9 %collective-permute-start.7 = (f32[32,100]{1,0:T(8,128)S(1)}, f32[32,100]{1,0:T(8,128)S(1)}, u32[]{:S(2)}, u32[]{:S(2)}) collective-permute-start(f32[32,100]{1,0:T(8,128)S(1)} %add.55), channel_id=1, source_target_pairs={{0,48},{1,49},{2,50},{3,51},{4,52},{5,53},{6,54},{7,55},{8,56},{9,... | collective-permute-start | bytes 38408 | tf_op jit(solution)/shard_map/ppermute | solution.py:39
  38.4 3.7 %collective-permute-start.8 = (f32[32,100]{1,0:T(8,128)S(1)}, f32[32,100]{1,0:T(8,128)S(1)}, u32[]{:S(2)}, u32[]{:S(2)}) collective-permute-start(f32[32,100]{1,0:T(8,128)S(1)} %add.56), channel_id=1, source_target_pairs={{0,4},{1,5},{2,6},{3,7},{4,0},{5,1},{6,2},{7,3},{8,12},{9,13},{10,... | collective-permute-start | bytes 38408 | tf_op jit(solution)/shard_map/ppermute | solution.py:39
  42.2 3.7 %collective-permute-start.9 = (f32[32,100]{1,0:T(8,128)S(1)}, f32[32,100]{1,0:T(8,128)S(1)}, u32[]{:S(2)}, u32[]{:S(2)}) collective-permute-start(f32[32,100]{1,0:T(8,128)S(1)} %add.57), channel_id=1, source_target_pairs={{0,1},{1,0},{2,3},{3,2},{4,5},{5,4},{6,7},{7,6},{8,9},{9,8},{10,11... | collective-permute-start | bytes 38408 | tf_op jit(solution)/shard_map/ppermute | solution.py:39
  45.9 4.9 %collective-permute-start.10 = (f32[32,100]{1,0:T(8,128)S(1)}, f32[32,100]{1,0:T(8,128)S(1)}, u32[]{:S(2)}, u32[]{:S(2)}) collective-permute-start(f32[32,100]{1,0:T(8,128)S(1)} %add.58), channel_id=1, source_target_pairs={{0,3},{1,2},{2,1},{3,0},{4,7},{5,6},{6,5},{7,4},{8,11},{9,10},{10,... | collective-permute-start | bytes 38408 | tf_op jit(solution)/shard_map/ppermute | solution.py:39
  55.3 3.4 %collective-permute-start.11 = (f32[3,4,1024]{2,1,0:T(4,128)S(1)}, f32[3,4,1024]{2,1,0:T(4,128)S(1)}, u32[]{:S(2)}, u32[]{:S(2)}) collective-permute-start(f32[3,4,1024]{2,1,0:T(4,128)S(1)} %get-tuple-element.69), channel_id=1, source_target_pairs={{0,8},{1,9},{2,10},{3,11},{4,12},{5,13},{6,14},{7,15},{8,0},{9,1},... | collective-permute-start | bytes 147464 | tf_op jit(solution)/shard_map/ppermute | solution.py:39
  55.3 5.7 %collective-permute-start.12 = (f32[3,4,1024]{2,1,0:T(4,128)S(1)}, f32[3,4,1024]{2,1,0:T(4,128)S(1)}, u32[]{:S(2)}, u32[]{:S(2)}) collective-permute-start(f32[3,4,1024]{2,1,0:T(4,128)S(1)} %get-tuple-element.70), channel_id=1, source_target_pairs={{0,64},{1,65},{2,66},{3,67},{4,68},{5,69},{6,70},{7,71},{8,72},{9,... | collective-permute-start | bytes 147464 | tf_op jit(solution)/shard_map/ppermute | solution.py:39
  58.5 5.2 %collective-permute-start.13 = (f32[3,4,1024]{2,1,0:T(4,128)S(1)}, f32[3,4,1024]{2,1,0:T(4,128)S(1)}, u32[]{:S(2)}, u32[]{:S(2)}) collective-permute-start(f32[3,4,1024]{2,1,0:T(4,128)S(1)} %get-tuple-element.71), channel_id=1, source_target_pairs={{0,72},{1,73},{2,74},{3,75},{4,76},{5,77},{6,78},{7,79},{8,64},{9,... | collective-permute-start | bytes 147464 | tf_op jit(solution)/shard_map/ppermute | solution.py:39
where the time goes:
time: 65.6 us; the launch traced here: 64.4 us
  Pallas kernels  25.7 us (39%)
  starting transfers between devices  22.1 us (34%)
  waiting for transfers between devices  11.2 us (17%)
  other arithmetic  2.39 us (4%)
  local copies, waits for them, and re-layouts  2.21 us (3%)
  between operations  0.74 us (1%)
    ppermute x14, starting transfers between devices, send(): return lax.ppermute(x, AXES, pairs_of(move))  22.1 us
    ppermute x14, waiting for transfers between devices, send(): return lax.ppermute(x, AXES, pairs_of(move))  11.2 us
    pallas_call x1, Pallas kernels, shards(): pl.pallas_call(forward_kernel, out_shape=(hb(TG, CLASSES), vm(*flat), vm(...  9.38 us
    pallas_call x1, Pallas kernels, shards(): pl.pallas_call(spread_kernel, out_shape=(vm(*spread_shape),) * 3, in_spec...  7.13 us
    pallas_call x5, Pallas kernels, near_call(): pl.pallas_call(kernel, out_shape=tuple((vm(*o) for o in outs)), in_specs=...  4.83 us
    pallas_call x1, Pallas kernels, shards(): pl.pallas_call(sum_kernel, out_shape=(hb(8, CLASSES),) + (hb(3, 4, PIXELS...  4.41 us
  transfers between devices with their start and end apart: 14, of which 7 were waited for; matrix products, arithmetic and copies ran while one was open for 6% of the time, Pallas kernels for 19%

commit v1 on v0

v1 whole, which is shorter than its diff:
```python
import math

import jax
import jax.numpy as jnp
import numpy as np
from jax import lax
from jax.experimental import pallas as pl
from jax.experimental.pallas import tpu as pltpu
from jax.sharding import PartitionSpec as P

SIDE = 32
CLASSES = 100
PIXELS = 1024
BETA = 0.01
TG = 32
SG = 8
ROWS = 8
DEEP = 16
AXES = ("tgt", "sup")
DIMS = (2, 4, 2, 2, 4)

TOP = (2.4493771255467647, 0.1932864690474489, -0.013754684085600787)
BOTTOM = (2.431483473487932, 3.4797192205950016)

VMEM = pl.BlockSpec(memory_space=pltpu.VMEM)
SMEM = pl.BlockSpec(memory_space=pltpu.SMEM)
F32 = jnp.float32


def pairs_of(move):
    out = []
    for src in range(int(np.prod(DIMS))):
        at = [int(v) for v in np.unravel_index(src, DIMS)]
        out.append((src, int(np.ravel_multi_index(move(*at), DIMS))))
    return out


def send(x, move):
    return lax.ppermute(x, AXES, pairs_of(move))


def even(v):
    return v ^ 1


def odd(v):
    return 3 - v


STEPS = (
    lambda yh, z, c, yl, x: (yh, even(z), c, yl, x),
    lambda yh, z, c, yl, x: (yh, odd(z), c, yl, x),
    lambda yh, z, c, yl, x: (yh, z, c, 1 - yl, x),
    lambda yh, z, c, yl, x: (yh, z, c, yl, even(x)),
    lambda yh, z, c, yl, x: (yh, z, c, yl, odd(x)),
)


def far_z(yh, z, c, yl, x):
    return (yh, z ^ 2, c, yl, x)


def far_x(yh, z, c, yl, x):
    return (yh, z, c, yl, x ^ 2)


def other_core(yh, z, c, yl, x):
    return (yh, z, 1 - c, yl, x)


def other_y(yh, z, c, yl, x):
    return (1 - yh, z, c, yl, x)


def rows_sum(v):
    lane = lax.broadcasted_iota(jnp.int32, v.shape[1:], 1)
    above = jnp.where(lane >= TG, pltpu.roll(v[ROWS - 1], TG, 1), 0.0)
    below = jnp.where(lane < 128 - TG, pltpu.roll(v[0], 128 - TG, 1), 0.0)
    line = [above] + [v[i] for i in range(ROWS)] + [below]
    out = []
    for i in range(1, ROWS + 1, 2):
        both = line[i] + line[i + 1]
        out += [line[i - 1] + both, both + line[i + 2]]
    return jnp.stack(out)


def down(v):
    return jnp.concatenate([rows_sum(v[:ROWS]), rows_sum(v[ROWS:])], axis=0)


def target_box(v):
    col = lax.broadcasted_iota(jnp.int32, v.shape, 1)
    v = v + jnp.where(col == 0, 0.0, pltpu.roll(v, 1, 1)) + jnp.where(col == SIDE - 1, 0.0, pltpu.roll(v, SIDE - 1, 1))
    return rows_sum(v)


def columns(ref, k):
    first, left, right, last = [ref[pl.ds(2 * k + n, 1)][0] for n in range(4)]
    both = left + right
    return ((2 * k, first + both), (2 * k + 1, both + last))


def wide(ref, k, j):
    one = jnp.broadcast_to(ref[k, :, pl.ds(j, 1), :], (ROWS, SG, 128))
    return jnp.concatenate([one, one], axis=0)


def pixel_box(v):
    lane = lax.broadcasted_iota(jnp.int32, v.shape, 1)
    col = lane & (SIDE - 1)
    v = v + jnp.where(col == 0, 0.0, pltpu.roll(v, 1, 1)) + jnp.where(col == SIDE - 1, 0.0, pltpu.roll(v, PIXELS - 1, 1))
    above = jnp.where(lane < SIDE, 0.0, pltpu.roll(v, SIDE, 1))
    below = jnp.where(lane >= PIXELS - SIDE, 0.0, pltpu.roll(v, PIXELS - SIDE, 1))
    return v + above + below


def spread_kernel(s_ref, y_ref, rb_ref, sb_ref, q_ref):
    def keep(k, v):
        for i in range(ROWS):
            row = jnp.concatenate([v[:, q * 256 + i * SIDE : q * 256 + (i + 1) * SIDE] for q in range(4)], axis=1)
            for g in range(2):
                q_ref[k, (g * ROWS + i) * SG : (g * ROWS + i + 1) * SG] = row[g * SG : (g + 1) * SG]

    energy = None
    for c in range(3):
        image = s_ref[c]
        energy = image * image if energy is None else energy + image * image
        keep(c, image * (1.0 / 27.0))
    level = pixel_box(energy * (1.0 / 27.0)) + BETA
    for l in range(3):
        inverse = lax.rsqrt(level)
        keep(3 + l, inverse)
        if l < 2:
            level = pixel_box(level * (1.0 / 9.0)) + BETA

    first = lax.broadcasted_iota(jnp.int32, (DEEP * SG, 128), 1) // TG * SIDE

    def body(j, carry):
        for k in range(6):
            one = jnp.take_along_axis(q_ref[k], first + j, axis=1).reshape(1, DEEP, SG, 128)
            if k < 3:
                y_ref[k, pl.ds(j, 1)] = one
            else:
                rb_ref[k - 3, pl.ds(j, 1)] = one
                sb_ref[k - 3, pl.ds(j, 1)] = lax.rsqrt(one * one) * (1.0 / 9.0)
        return carry

    lax.fori_loop(0, SIDE, body, 0, unroll=2)


def spread(ref, k, j):
    return ref[k, pl.ds(j, 1)][0]


def own_duals(place_ref, dual_ref):
    return [dual_ref[pl.ds(place_ref[4 + k] * 4, 4), :] for k in range(4)]


def forward_kernel(
    place_ref, x_ref, y_ref, rb_ref, sb_ref, dual_ref, label_ref,
    pred_ref, xt_ref, h0_ref, h1_ref, w0_ref, w1_ref, w2_ref, v2_ref,
    ra_ref, sa_ref, va_ref, vb_ref,
):
    energy = None
    for c in range(3):
        parts = []
        for q in range(4):
            for r in range(4):
                parts.append(x_ref[r, c * 8 : (c + 1) * 8, q * 256 : (q + 1) * 256])
        turned = jnp.concatenate(parts, axis=0).T.reshape(ROWS, SIDE, 128)
        xt_ref[c] = turned
        energy = turned * turned if energy is None else energy + turned * turned
    level = target_box(energy * (1.0 / 27.0)) + BETA
    for l in range(3):
        inverse = lax.rsqrt(level)
        ra_ref[l] = inverse
        sa_ref[l] = level * inverse * (1.0 / math.pi)
        if l < 2:
            level = target_box(level * (1.0 / 9.0)) + BETA

    clear_edges(va_ref, vb_ref, v2_ref)

    def inner(j, carry):
        total = spread(y_ref, 0, j) * wide(xt_ref, 0, j)
        total = total + spread(y_ref, 1, j) * wide(xt_ref, 1, j)
        total = total + spread(y_ref, 2, j) * wide(xt_ref, 2, j)
        va_ref[pl.ds(j + 1, 1)] = down(total)[None]
        return carry

    lax.fori_loop(0, SIDE, inner, 0, unroll=2)

    def layer(l, j, around):
        cross = around + BETA
        x = cross * (spread(rb_ref, l, j) * wide(ra_ref, l, j))
        u = jnp.abs(x) if l == 0 else x
        d = jnp.maximum(1.0 - u * u, 1e-30)
        s = d * lax.rsqrt(d)
        top = (u * (TOP[2] / (9.0 * math.pi)) + TOP[1] / (9.0 * math.pi)) * u + TOP[0] / (9.0 * math.pi)
        q = s * (top * lax.rsqrt((u + BOTTOM[1]) * u + BOTTOM[0]))
        h = 1.0 / 9.0 - q
        if l == 0:
            h = jnp.where(x >= 0.0, h, q)
        w = (spread(sb_ref, l, j) * wide(sa_ref, l, j)) * s
        return h, w, w + h * cross

    def layer0(k, carry):
        for j, around in columns(va_ref, k):
            h, w, f = layer(0, j, around)
            h0_ref[pl.ds(j, 1)] = h[None]
            w0_ref[pl.ds(j, 1)] = w[None]
            vb_ref[pl.ds(j + 1, 1)] = down(f)[None]
        return carry

    def layer1(k, carry):
        for j, around in columns(vb_ref, k):
            h, w, f = layer(1, j, around)
            h1_ref[pl.ds(j, 1)] = h[None]
            w1_ref[pl.ds(j, 1)] = w[None]
            va_ref[pl.ds(j + 1, 1)] = down(f)[None]
        return carry

    def layer2(k, total):
        for j, around in columns(va_ref, k):
            h, w, f = layer(2, j, around)
            w2_ref[pl.ds(j, 1)] = w[None]
            v2_ref[pl.ds(j + 1, 1)] = down(h)[None]
            total = total + jnp.sum(f.reshape(2, ROWS, SG, 128), axis=1)
        return total

    lax.fori_loop(0, SIDE // 2, layer0, 0, unroll=2)
    lax.fori_loop(0, SIDE // 2, layer1, 0, unroll=2)
    total = lax.fori_loop(0, SIDE // 2, layer2, jnp.zeros((2, SG, 128), F32), unroll=2)
    kernel = total * (9.0 / PIXELS)
    duals = own_duals(place_ref, dual_ref)
    wide_pred = None
    for g in range(2):
        part = lax.dot_general(
            kernel[g], jnp.concatenate(duals[2 * g : 2 * g + 2], axis=0), (((0,), (0,)), ((), ())),
            precision=lax.Precision.HIGHEST, preferred_element_type=F32,
        )
        wide_pred = part if wide_pred is None else wide_pred + part
    pred = wide_pred[:32] + wide_pred[32:64] + wide_pred[64:96] + wide_pred[96:]
    for r in range(4):
        rows = pred[r * 8 : (r + 1) * 8]
        if r == 0:
            row = lax.broadcasted_iota(jnp.int32, rows.shape, 0)
            own = jnp.zeros(rows.shape, jnp.int32)
            for t in range(8):
                own = jnp.where(row == t, label_ref[t], own)
            hot = (own == lax.broadcasted_iota(jnp.int32, rows.shape, 1)) & (place_ref[8] == 0)
            rows = rows - jnp.where(hot, 1.0, 0.0)
        pred_ref[pl.ds(pl.multiple_of(place_ref[r] * 8, 8), 8), :] = rows


def clear_edges(*refs):
    for ref in refs:
        ref[0] = jnp.zeros((DEEP, SG, 128), F32)
        ref[SIDE + 1] = jnp.zeros((DEEP, SG, 128), F32)


def at(ref, j):
    return ref[pl.ds(j, 1)][0]


def back_kernel_a(v2_ref, h1_ref, w1_ref, w2_ref, h0_ref, w0_ref, rb_ref, v0_ref, l0_ref, p1_ref, l1_ref, v1_ref, p2_ref):
    clear_edges(v1_ref, p2_ref, v0_ref, p1_ref)

    def layer1(k, carry):
        for j, up in columns(v2_ref, k):
            rb = spread(rb_ref, 1, j)
            l1_ref[pl.ds(j, 1)] = (up * at(w1_ref, j) * (rb * rb))[None]
            v1_ref[pl.ds(j + 1, 1)] = down(up * at(h1_ref, j))[None]
            rb = spread(rb_ref, 2, j)
            p2_ref[pl.ds(j + 1, 1)] = down(at(w2_ref, j) * (rb * rb))[None]
        return carry

    def layer0(k, carry):
        for (j, up), (_, sums) in zip(columns(v1_ref, k), columns(p2_ref, k)):
            rb = spread(rb_ref, 0, j)
            l0_ref[pl.ds(j, 1)] = (up * at(w0_ref, j) * (rb * rb))[None]
            v0_ref[pl.ds(j + 1, 1)] = down(up * at(h0_ref, j))[None]
            p1_ref[pl.ds(j + 1, 1)] = down(at(l1_ref, j) + sums * (1.0 / 9.0))[None]
        return carry

    lax.fori_loop(0, SIDE // 2, layer1, 0, unroll=2)
    lax.fori_loop(0, SIDE // 2, layer0, 0, unroll=2)


def back_kernel_b(l0_ref, p1_ref, p0_ref):
    clear_edges(p0_ref)

    def body(k, carry):
        for j, sums in columns(p1_ref, k):
            p0_ref[pl.ds(j + 1, 1)] = down(at(l0_ref, j) + sums * (1.0 / 9.0))[None]
        return carry

    lax.fori_loop(0, SIDE // 2, body, 0, unroll=2)


def back_kernel_c(v0_ref, p0_ref, xt_ref, y_ref, g_ref):
    def body(k, carry):
        for (j, up), (_, energy) in zip(columns(v0_ref, k), columns(p0_ref, k)):
            energy = energy * 27.0
            for c in range(3):
                g_ref[c, pl.ds(j, 1)] = (up * wide(xt_ref, c, j) + energy * spread(y_ref, c, j))[None]
        return carry

    lax.fori_loop(0, SIDE // 2, body, 0)


def sum_kernel(place_ref, res_ref, dual_ref, g_ref, own_ref, *out_refs):
    own_ref[...] = res_ref[pl.ds(pl.multiple_of(place_ref[0] * 8, 8), 8), :]
    rows = [res_ref[pl.ds(pl.multiple_of(place_ref[r] * 8, 8), 8), :] for r in range(4)]
    weight = lax.dot_general(
        jnp.concatenate(own_duals(place_ref, dual_ref), axis=0) * (1.0 / 3.0), jnp.concatenate(rows * 4, axis=0), (((1,), (1,)), ((), ())),
        precision=lax.Precision.HIGHEST, preferred_element_type=F32,
    )
    weight = jnp.broadcast_to(weight.reshape(2, 1, SG, 128), (2, ROWS, SG, 128)).reshape(DEEP, SG, 128)
    row = lax.broadcasted_iota(jnp.int32, (512, 128), 0)
    col = lax.broadcasted_iota(jnp.int32, (512, 128), 1)
    place = col - (row & 127) // TG * SIDE - lax.shift_right_logical(row, 7)
    total = jnp.zeros((3 * 128, 128), F32)
    for j in range(0, SIDE, 4):
        pick = jnp.where(place == j, 1.0, 0.0).astype(jnp.bfloat16)
        his, lows = [], []
        for k in range(4):
            term = (g_ref[:, j + k] * weight).reshape(3 * 128, 128)
            hi = term.astype(jnp.bfloat16)
            his.append(hi)
            lows.append((term - hi.astype(F32)).astype(jnp.bfloat16))
        total = total + jnp.dot(jnp.concatenate(his, axis=1), pick, preferred_element_type=F32)
        total = total + jnp.dot(jnp.concatenate(lows, axis=1), pick, preferred_element_type=F32)
    for c in range(3):
        for g in range(2):
            image = [total[((c * 2 + g) * ROWS + i) * SG : ((c * 2 + g) * ROWS + i + 1) * SG] for i in range(ROWS)]
            line = jnp.concatenate([image[i][:, q * SIDE : (q + 1) * SIDE] for q in range(4) for i in range(ROWS)], axis=1)
            out_refs[0][c, g * 4 : g * 4 + 4] = line[:4]
            out_refs[1][c, g * 4 : g * 4 + 4] = line[4:]


def near(x):
    return pltpu.with_memory_space_constraint(x, pltpu.VMEM)


def vm(*shape):
    return pltpu.VMEM(shape, F32)


def hb(*shape):
    return jax.ShapeDtypeStruct(shape, F32)


def params(mib):
    return pltpu.CompilerParams(vmem_limit_bytes=mib << 20)


def shards(target_pool, target_index, target_labels, dual_weights, support_images):
    tgt = lax.axis_index("tgt")
    sup = lax.axis_index("sup")
    z = (tgt // 2) % 4

    mine = support_images.transpose(1, 0, 2)
    pair = jnp.concatenate([mine, send(mine, other_core)], axis=1)
    target_index, pair = lax.optimization_barrier((target_index, pair))
    support = jnp.concatenate([pair, send(pair, other_y)], axis=1)
    rows = (target_index - tgt * target_pool.shape[0]).astype(jnp.uint32)
    targets = target_pool.at[rows].get(mode="promise_in_bounds")
    block = targets.transpose(1, 0, 2).reshape(24, PIXELS)
    x_all = jnp.stack([block, send(block, STEPS[0]), send(block, STEPS[1]), send(block, far_z)])
    place = jnp.stack([z, z ^ 1, 3 - z, z ^ 2] + [tgt ^ k for k in (0, 1, 8, 9)] + [sup]).astype(jnp.int32)

    spread_shape = (3, SIDE, DEEP, SG, 128)
    y_wide, rb_wide, sb_wide = pl.pallas_call(
        spread_kernel, out_shape=(vm(*spread_shape),) * 3, in_specs=[VMEM], out_specs=(VMEM,) * 3,
        scratch_shapes=[pltpu.VMEM((6, DEEP * SG, 128), F32)], compiler_params=params(6), name="spread",
    )(support)

    column = (SIDE, DEEP, SG, 128)
    padded = (SIDE + 2, DEEP, SG, 128)
    flat = (3, ROWS, SIDE, 128)

    def near_call(kernel, outs, ins, name, scratch=(), mib=6):
        return pl.pallas_call(
            kernel, out_shape=tuple(vm(*o) for o in outs), in_specs=[VMEM] * len(ins), out_specs=(VMEM,) * len(outs),
            scratch_shapes=[pltpu.VMEM(v, F32) for v in scratch], compiler_params=params(mib), name=name,
        )(*map(near, ins))

    pred, xt, h0, h1, w0, w1, w2, v2 = pl.pallas_call(
        forward_kernel,
        out_shape=(hb(TG, CLASSES), vm(*flat), vm(*column), vm(*column), vm(*column), vm(*column), vm(*column), vm(*padded)),
        in_specs=[SMEM] + [VMEM] * 5 + [SMEM],
        out_specs=(VMEM,) * 8,
        scratch_shapes=[pltpu.VMEM(flat, F32), pltpu.VMEM(flat, F32), pltpu.VMEM(padded, F32), pltpu.VMEM(padded, F32)],
        compiler_params=params(14), name="forward",
    )(place, x_all, near(y_wide), near(rb_wide), near(sb_wide), dual_weights, target_labels)

    def around(res, moves):
        near_a, near_b, far = [send(res, move) for move in moves]
        return lambda: (res + near_a) + (near_b + far)

    res, v2 = lax.optimization_barrier((pred, v2))
    added = around(res, (STEPS[0], STEPS[1], far_z))
    v0, l0, p1 = near_call(
        back_kernel_a, (padded, column, padded), (v2, h1, w1, w2, h0, w0, rb_wide), "back_a",
        scratch=(column, padded, padded), mib=9,
    )
    res, l0 = lax.optimization_barrier((added(), l0))
    new = send(res, STEPS[2])
    (p0,) = near_call(back_kernel_b, (padded,), (l0, p1), "back_b")
    res, p0 = lax.optimization_barrier((res + new, p0))
    added = around(res, (STEPS[3], STEPS[4], far_x))
    (g,) = near_call(back_kernel_c, ((3,) + column,), (v0, p0, xt, y_wide), "back_c")
    res = added()

    residual, *parts = pl.pallas_call(
        sum_kernel, out_shape=(hb(8, CLASSES),) + (hb(3, 8, PIXELS),) * 2,
        in_specs=[SMEM] + [VMEM] * 3, out_specs=(VMEM,) * 3,
        compiler_params=params(10), name="weighted",
    )(place, res, dual_weights, near(g))
    pair = parts[0] + send(parts[1], other_core)
    total = pair[:, :4] + send(pair[:, 4:], other_y)
    return (residual, total.transpose(1, 0, 2))


def solution(mesh):
    in_specs = (
        P("tgt", None, None),
        P("tgt"),
        P("tgt"),
        P("sup", None),
        P(("sup", "tgt"), None, None),
    )
    out_specs = (P("tgt", None), P(("sup", "tgt"), None, None))
    return jax.shard_map(shards, mesh=mesh, in_specs=in_specs, out_specs=out_specs, check_vma=False)
```

time: 65.6 us -> 59.2 us (0.902); the launches traced: 64.4 us -> 59 us
  starting transfers between devices: 22.1 us -> 18.4 us
  Pallas kernels: 25.7 us -> 22.4 us
  waiting for transfers between devices: 11.2 us -> 14.4 us
  local copies, waits for them, and re-layouts: 2.21 us -> 0.81 us
    ppermute x14, starting transfers between devices: 22.1 us -> 18.4 us  [send(): return lax.ppermute(x, AXES, pairs_of(move))]
    ppermute x14, waiting for transfers between devices: 11.2 us -> 14.4 us  [send(): return lax.ppermute(x, AXES, pairs_of(move))]
    pallas_call x1, Pallas kernels: 7.13 us -> 5.5 us  [shards(): pl.pallas_call(spread_kernel, out_shape=(vm(*spread_shape),) * 3, in_spec...]
    pallas_call x1, Pallas kernels: 4.41 us -> 3.39 us  [shards(): pl.pallas_call(sum_kernel, out_shape=(hb(8, CLASSES),) + (hb(3, 8, PIXELS...]
    dynamic_slice x1 -> x0, local copies, waits for them, and re-layouts: 0.77 us -> none  [shards(): lax.dynamic_slice_in_dim(dual_weights, (tgt ^ k) * 4, 4, 0)]
    select_n x1 -> x0, other arithmetic: 0.66 us -> none  [shards(): target_pool.at[target_index - tgt * target_pool.shape[0]]]
    convert_element_type x0 -> x1, other arithmetic: none -> 0.66 us  [shards(): targets = target_pool.at[rows].get(mode='promise_in_bounds')]
    pallas_call x5 -> x3, Pallas kernels: 4.83 us -> 4.4 us  [near_call(): pl.pallas_call(kernel, out_shape=tuple((vm(*o) for o in outs)), in_specs=...]
  transfers between devices with their start and end apart: 14 -> 14, of which waited for: 7 -> 6; matrix products, arithmetic and copies ran while one was open for 6% -> 2% of each run, Pallas kernels for 19% -> 17%
where the time goes in v1:
time: 59.2 us; the launch traced here: 59 us
  Pallas kernels  22.4 us (38%)
  starting transfers between devices  18.4 us (31%)
  waiting for transfers between devices  14.4 us (24%)
  other arithmetic  2.2 us (4%)
  between operations  0.82 us (1%)
  local copies, waits for them, and re-layouts  0.81 us (1%)
    ppermute x14, starting transfers between devices, send(): return lax.ppermute(x, AXES, pairs_of(move))  18.4 us
    ppermute x14, waiting for transfers between devices, send(): return lax.ppermute(x, AXES, pairs_of(move))  14.4 us
    pallas_call x1, Pallas kernels, shards(): pl.pallas_call(forward_kernel, out_shape=(hb(TG, CLASSES), vm(*flat), vm(...  9.15 us
    pallas_call x1, Pallas kernels, shards(): pl.pallas_call(spread_kernel, out_shape=(vm(*spread_shape),) * 3, in_spec...  5.5 us
    pallas_call x3, Pallas kernels, near_call(): pl.pallas_call(kernel, out_shape=tuple((vm(*o) for o in outs)), in_specs=...  4.4 us
    pallas_call x1, Pallas kernels, shards(): pl.pallas_call(sum_kernel, out_shape=(hb(8, CLASSES),) + (hb(3, 8, PIXELS...  3.39 us
  transfers between devices with their start and end apart: 14, of which 6 were waited for; matrix products, arithmetic and copies ran while one was open for 2% of the time, Pallas kernels for 17%

profile of v1, /device:TPU:0, one launch (start us, length us, event | category | flops | bytes accessed | tf_op | source)
XLA Modules:
  0.0 59.0 jit_solution(15702580308695454211)
XLA Ops:
  0.9 1.3 %collective-permute-done = f32[3,4,1024]{2,1,0:T(4,128)S(1)} collective-permute-done((f32[3,4,1024]{2,1,0:T(4,128)}, f32[3,4,1024]{2,1,0:T(4,128)S(1)}, u32[]{:S(2)}, u32[]{:S(2)}) %collective-permute-start) | collective-permute-done | bytes 49184 | tf_op jit(solution)/shard_map/ppermute | solution.py:39
  2.2 0.8 %pad_maximum_fusion.2 = f32[3,8,1024]{2,1,0:T(8,128)S(1)} fusion(f32[3,4,1024]{2,1,0:T(4,128)S(1)} %collective-permute-done, f32[3,4,1024]{2,1,0:T(4,128)} %bitcast.28), kind=kLoop, calls=%fused_computation.3 | loop fusion | flops 24576 | bytes 196608 | tf_op jit(solution)/shard_map/concatenate | solution.py:363
  3.0 3.4 %collective-permute-start.4 = (f32[3,8,1024]{2,1,0:T(8,128)S(1)}, f32[3,8,1024]{2,1,0:T(8,128)S(1)}, u32[]{:S(2)}, u32[]{:S(2)}) collective-permute-start(f32[3,8,1024]{2,1,0:T(8,128)S(1)} %pad_maximum_fusion.2), channel_id=1, source_target_pairs={{0,64},{1,65},{2,66},{3,67},{4,68},{5,69},{6,70},{7,71},{8,72},{9,... | collective-permute-start | bytes 294920 | tf_op jit(solution)/shard_map/ppermute | solution.py:39
  6.4 0.7 %convert_convert_fusion = s32[8]{0:T(128)S(1)} fusion(s32[8]{0:T(128)} %param.6, s32[]{:T(128)S(6)} %mul.3), kind=kLoop, calls=%fused_computation.9 | loop fusion | flops 24 | bytes 68 | tf_op jit(solution)/shard_map/convert_element_type | solution.py:367
  7.0 0.7 %gather_fusion = f32[8,3,1024]{2,0,1:T(8,128)S(1)} fusion(f32[64,3,1024]{2,0,1:T(8,128)S(1)} %copy-done, s32[1024]{0:T(1024)S(1)} %pad_clamp_fusion), kind=kCustom, calls=%fused_computation | custom fusion | bytes 196640 | tf_op jit(solution)/shard_map/gather | solution.py:367
  7.7 4.0 %collective-permute-start.3 = (f32[24,1024]{1,0:T(8,128)S(1)}, f32[24,1024]{1,0:T(8,128)S(1)}, u32[]{:S(2)}, u32[]{:S(2)}) collective-permute-start(f32[24,1024]{1,0:T(8,128)S(1)} %bitcast.20), channel_id=1, source_target_pairs={{0,32},{1,33},{2,34},{3,35},{4,36},{5,37},{6,38},{7,39},{8,40},{9,... | collective-permute-start | bytes 294920 | tf_op jit(solution)/shard_map/ppermute | solution.py:39
  11.7 0.7 %collective-permute-start.2 = (f32[24,1024]{1,0:T(8,128)S(1)}, f32[24,1024]{1,0:T(8,128)S(1)}, u32[]{:S(2)}, u32[]{:S(2)}) collective-permute-start(f32[24,1024]{1,0:T(8,128)S(1)} %bitcast.21), channel_id=1, source_target_pairs={{0,48},{1,49},{2,50},{3,51},{4,52},{5,53},{6,54},{7,55},{8,56},{9,... | collective-permute-start | bytes 294920 | tf_op jit(solution)/shard_map/ppermute | solution.py:39
  12.7 5.5 %spread.1 = (f32[3,32,16,8,128]{4,3,2,1,0:T(8,128)S(1)}, f32[3,32,16,8,128]{4,3,2,1,0:T(8,128)S(1)}, f32[3,32,16,8,128]{4,3,2,1,0:T(8,128)S(1)}) custom-call(f32[3,16,1024]{2,1,0:T(8,128)S(1)} %pad_maximum_fusion.1.s_ref), custom_call_target="tpu_custom_call" | custom-call | tf_op jit(solution)/shard_map/spread/pallas_call | solution.py:373
  18.3 9.2 %forward.1 = (f32[32,100]{1,0:T(8,128)S(1)}, f32[3,8,32,128]{3,2,1,0:T(8,128)S(1)}, f32[32,16,8,128]{3,2,1,0:T(8,128)S(1)}, f32[32,16,8,128]{3,2,1,0:T(8,128)S(1...) custom-call(s32[9]{0:T(128)S(1)} %stack.51.place_ref, ...), custom_call_target="tpu_custom_call" | custom-call | tf_op jit(solution)/shard_map/forward/pallas_call | solution.py:388
  27.5 3.7 %collective-permute-start.7 = (f32[32,100]{1,0:T(8,128)S(1)}, f32[32,100]{1,0:T(8,128)S(1)}, u32[]{:S(2)}, u32[]{:S(2)}) collective-permute-start(f32[32,100]{1,0:T(8,128)S(1)} %get-tuple-element.34), channel_id=1, source_target_pairs={{0,32},{1,33},{2,34},{3,35},{4,36},{5,37},{6,38},{7,39},{8,40},{9,... | collective-permute-start | bytes 38408 | tf_op jit(solution)/shard_map/ppermute | solution.py:39
  31.2 0.7 %collective-permute-start.6 = (f32[32,100]{1,0:T(8,128)S(1)}, f32[32,100]{1,0:T(8,128)S(1)}, u32[]{:S(2)}, u32[]{:S(2)}) collective-permute-start(f32[32,100]{1,0:T(8,128)S(1)} %get-tuple-element.34), channel_id=1, source_target_pairs={{0,48},{1,49},{2,50},{3,51},{4,52},{5,53},{6,54},{7,55},{8,56},{9,... | collective-permute-start | bytes 38408 | tf_op jit(solution)/shard_map/ppermute | solution.py:39
  31.9 2.1 %back_a.1 = (f32[34,16,8,128]{3,2,1,0:T(8,128)S(1)}, f32[32,16,8,128]{3,2,1,0:T(8,128)S(1)}, f32[34,16,8,128]{3,2,1,0:T(8,128)S(1)}) custom-call(f32[34,16,8,128]{3,2,1,0:T(8,128)S(1)} %get-tuple-element.35.v2_ref, f32[32,16,8,128]{3,2,1,0:T(8,128)S(1)} %get-tuple-element.36.h1_ref, f32[32,16,8,128]{3,2,1,0:T(8,128)S(1)} %get-tuple-element.37.w1_ref, ...), custom_call_target="tpu_custom_call" | custom-call | tf_op jit(solution)/shard_map/back_a/pallas_call | solution.py:383
  34.1 2.1 %collective-permute-done.6 = f32[32,100]{1,0:T(8,128)S(1)} collective-permute-done((f32[32,100]{1,0:T(8,128)S(1)}, f32[32,100]{1,0:T(8,128)S(1)}, u32[]{:S(2)}, u32[]{:S(2)}) %collective-permute-start.6) | collective-permute-done | bytes 12832 | tf_op jit(solution)/shard_map/ppermute | solution.py:39
  36.2 0.8 %collective-permute-start.8 = (f32[32,100]{1,0:T(8,128)S(1)}, f32[32,100]{1,0:T(8,128)S(1)}, u32[]{:S(2)}, u32[]{:S(2)}) collective-permute-start(f32[32,100]{1,0:T(8,128)S(1)} %add_add_fusion.1), channel_id=1, source_target_pairs={{0,4},{1,5},{2,6},{3,7},{4,0},{5,1},{6,2},{7,3},{8,12},{9,13},{10,... | collective-permute-start | bytes 38408 | tf_op jit(solution)/shard_map/ppermute | solution.py:39
  36.9 0.8 %back_b.1.p0_ref = f32[34,16,8,128]{3,2,1,0:T(8,128)S(1)} custom-call(f32[32,16,8,128]{3,2,1,0:T(8,128)S(1)} %get-tuple-element.43.l0_ref, f32[34,16,8,128]{3,2,1,0:T(8,128)S(1)} %get-tuple-element.44.p1_ref), custom_call_target="tpu_custom_call" | custom-call | tf_op jit(solution)/shard_map/back_b/pallas_call | solution.py:383
  37.7 2.3 %collective-permute-done.8 = f32[32,100]{1,0:T(8,128)S(1)} collective-permute-done((f32[32,100]{1,0:T(8,128)S(1)}, f32[32,100]{1,0:T(8,128)S(1)}, u32[]{:S(2)}, u32[]{:S(2)}) %collective-permute-start.8) | collective-permute-done | bytes 12832 | tf_op jit(solution)/shard_map/ppermute | solution.py:39
  40.0 3.0 %collective-permute-start.11 = (f32[32,100]{1,0:T(8,128)S(1)}, f32[32,100]{1,0:T(8,128)S(1)}, u32[]{:S(2)}, u32[]{:S(2)}) collective-permute-start(f32[32,100]{1,0:T(8,128)S(1)} %add.36), channel_id=1, source_target_pairs={{0,2},{1,3},{2,0},{3,1},{4,6},{5,7},{6,4},{7,5},{8,10},{9,11},{10,... | collective-permute-start | bytes 38408 | tf_op jit(solution)/shard_map/ppermute | solution.py:39
  43.0 1.1 %collective-permute-start.10 = (f32[32,100]{1,0:T(8,128)S(1)}, f32[32,100]{1,0:T(8,128)S(1)}, u32[]{:S(2)}, u32[]{:S(2)}) collective-permute-start(f32[32,100]{1,0:T(8,128)S(1)} %add.36), channel_id=1, source_target_pairs={{0,3},{1,2},{2,1},{3,0},{4,7},{5,6},{6,5},{7,4},{8,11},{9,10},{10,... | collective-permute-start | bytes 38408 | tf_op jit(solution)/shard_map/ppermute | solution.py:39
  44.2 1.5 %back_c.1.g_ref = f32[3,32,16,8,128]{4,3,2,1,0:T(8,128)S(1)} custom-call(f32[34,16,8,128]{3,2,1,0:T(8,128)S(1)} %get-tuple-element.46.v0_ref, f32[34,16,8,128]{3,2,1,0:T(8,128)S(1)} %back_b.1.p0_ref, f32[3,8,32,128]{3,2,1,0:T(8,128)S(1)} %get-tuple-element.48.xt_ref, f32[3,32,16,8,128]{4,3,2,1,0:T(8,128)S(1)} %get-tuple-element.29.y_ref), custom_call_target="tpu_custom_call" | custom-call | tf_op jit(solution)/shard_map/back_c/pallas_call | solution.py:383
  45.7 2.3 %collective-permute-done.10 = f32[32,100]{1,0:T(8,128)S(1)} collective-permute-done((f32[32,100]{1,0:T(8,128)S(1)}, f32[32,100]{1,0:T(8,128)S(1)}, u32[]{:S(2)}, u32[]{:S(2)}) %collective-permute-start.10) | collective-permute-done | bytes 12832 | tf_op jit(solution)/shard_map/ppermute | solution.py:39
  48.0 3.4 %weighted.1 = (f32[8,100]{1,0:T(8,128)}, f32[3,8,1024]{2,1,0:T(8,128)S(1)}, f32[3,8,1024]{2,1,0:T(8,128)S(1)}) custom-call(s32[9]{0:T(128)S(1)} %stack.51.place_ref, f32[32,100]{1,0:T(8,128)S(1)} %add_add_fusion.res_ref, f32[64,100]{1,0:T(8,128)S(1)} %copy-done.1, f32[3,32,16,8,128]{4,3,2,1,0:T(8,128)S(1)} %back_c.1.g_ref), custom_call_target="tpu_custom_call" | custom-call | tf_op jit(solution)/shard_map/weighted/pallas_call | solution.py:415
  51.4 1.3 %collective-permute-done.12 = f32[3,8,1024]{2,1,0:T(8,128)S(1)} collective-permute-done((f32[3,8,1024]{2,1,0:T(8,128)S(1)}, f32[3,8,1024]{2,1,0:T(8,128)S(1)}, u32[]{:S(2)}, u32[]{:S(2)}) %collective-permute-start.12) | collective-permute-done | bytes 98336 | tf_op jit(solution)/shard_map/ppermute | solution.py:39
  53.3 5.1 %collective-permute-done.13 = f32[3,4,1024]{2,1,0:T(4,128)S(1)} collective-permute-done((f32[3,4,1024]{2,1,0:T(4,128)S(1)}, f32[3,4,1024]{2,1,0:T(4,128)S(1)}, u32[]{:S(2)}, u32[]{:S(2)}) %collective-permute-start.13) | collective-permute-done | bytes 49184 | tf_op jit(solution)/shard_map/ppermute | solution.py:39
  58.4 0.6 %fusion = f32[4,3,1024]{2,0,1:T(4,128)} fusion(f32[3,4,1024]{2,1,0:T(4,128)S(1)} %collective-permute-done.13, f32[3,8,1024]{2,1,0:T(8,128)S(1)} %add.40), kind=kLoop, calls=%fused_computation.5 | loop fusion | flops 12288 | bytes 147456 | tf_op jit(solution)/shard_map/transpose | solution.py:422
  (29 shorter events, 1.2 us)
Async XLA Ops:
  0.6 6.4 %copy-start = (f32[64,3,1024]{2,0,1:T(8,128)S(1)}, f32[64,3,1024]{2,0,1:T(8,128)}, u32[]{:S(2)}) copy-start(f32[64,3,1024]{2,0,1:T(8,128)} %param.5) | copy-start | bytes 2359300
  0.6 17.7 %copy-start.1 = (f32[64,100]{1,0:T(8,128)S(1)}, f32[64,100]{1,0:T(8,128)}, u32[]{:S(2)}) copy-start(f32[64,100]{1,0:T(8,128)} %dual_ref.3) | copy-start | bytes 76804
  0.7 17.7 %copy-start.2 = (s32[8]{0:T(128)S(1)}, s32[8]{0:T(128)}, u32[]{:S(2)}) copy-start(s32[8]{0:T(128)} %label_ref.1) | copy-start | bytes 100
  0.7 1.5 %collective-permute-start = (f32[3,4,1024]{2,1,0:T(4,128)}, f32[3,4,1024]{2,1,0:T(4,128)S(1)}, u32[]{:S(2)}, u32[]{:S(2)}) collective-permute-start(f32[3,4,1024]{2,1,0:T(4,128)} %bitcast.27), channel_id=1, source_target_pairs={{0,8},{1,9},{2,10},{3,11},{4,12},{5,13},{6,14},{7,15},{8,0},{9,1},... | collective-permute-start | bytes 147464 | tf_op jit(solution)/shard_map/ppermute | solution.py:39
  3.0 9.7 %collective-permute-start.4 = (f32[3,8,1024]{2,1,0:T(8,128)S(1)}, f32[3,8,1024]{2,1,0:T(8,128)S(1)}, u32[]{:S(2)}, u32[]{:S(2)}) collective-permute-start(f32[3,8,1024]{2,1,0:T(8,128)S(1)} %pad_maximum_fusion.2), channel_id=1, source_target_pairs={{0,64},{1,65},{2,66},{3,67},{4,68},{5,69},{6,70},{7,71},{8,72},{9,... | collective-permute-start | bytes 294920 | tf_op jit(solution)/shard_map/ppermute | solution.py:39
  7.7 10.5 %collective-permute-start.3 = (f32[24,1024]{1,0:T(8,128)S(1)}, f32[24,1024]{1,0:T(8,128)S(1)}, u32[]{:S(2)}, u32[]{:S(2)}) collective-permute-start(f32[24,1024]{1,0:T(8,128)S(1)} %bitcast.20), channel_id=1, source_target_pairs={{0,32},{1,33},{2,34},{3,35},{4,36},{5,37},{6,38},{7,39},{8,40},{9,... | collective-permute-start | bytes 294920 | tf_op jit(solution)/shard_map/ppermute | solution.py:39
  11.7 6.6 %collective-permute-start.2 = (f32[24,1024]{1,0:T(8,128)S(1)}, f32[24,1024]{1,0:T(8,128)S(1)}, u32[]{:S(2)}, u32[]{:S(2)}) collective-permute-start(f32[24,1024]{1,0:T(8,128)S(1)} %bitcast.21), channel_id=1, source_target_pairs={{0,48},{1,49},{2,50},{3,51},{4,52},{5,53},{6,54},{7,55},{8,56},{9,... | collective-permute-start | bytes 294920 | tf_op jit(solution)/shard_map/ppermute | solution.py:39
  12.4 5.9 %collective-permute-start.1 = (f32[24,1024]{1,0:T(8,128)S(1)}, f32[24,1024]{1,0:T(8,128)S(1)}, u32[]{:S(2)}, u32[]{:S(2)}) collective-permute-start(f32[24,1024]{1,0:T(8,128)S(1)} %bitcast.22), channel_id=1, source_target_pairs={{0,16},{1,17},{2,18},{3,19},{4,20},{5,21},{6,22},{7,23},{8,24},{9,... | collective-permute-start | bytes 294920 | tf_op jit(solution)/shard_map/ppermute | solution.py:39
  27.5 6.6 %collective-permute-start.7 = (f32[32,100]{1,0:T(8,128)S(1)}, f32[32,100]{1,0:T(8,128)S(1)}, u32[]{:S(2)}, u32[]{:S(2)}) collective-permute-start(f32[32,100]{1,0:T(8,128)S(1)} %get-tuple-element.34), channel_id=1, source_target_pairs={{0,32},{1,33},{2,34},{3,35},{4,36},{5,37},{6,38},{7,39},{8,40},{9,... | collective-permute-start | bytes 38408 | tf_op jit(solution)/shard_map/ppermute | solution.py:39
  31.2 4.9 %collective-permute-start.6 = (f32[32,100]{1,0:T(8,128)S(1)}, f32[32,100]{1,0:T(8,128)S(1)}, u32[]{:S(2)}, u32[]{:S(2)}) collective-permute-start(f32[32,100]{1,0:T(8,128)S(1)} %get-tuple-element.34), channel_id=1, source_target_pairs={{0,48},{1,49},{2,50},{3,51},{4,52},{5,53},{6,54},{7,55},{8,56},{9,... | collective-permute-start | bytes 38408 | tf_op jit(solution)/shard_map/ppermute | solution.py:39
  31.9 4.2 %collective-permute-start.5 = (f32[32,100]{1,0:T(8,128)S(1)}, f32[32,100]{1,0:T(8,128)S(1)}, u32[]{:S(2)}, u32[]{:S(2)}) collective-permute-start(f32[32,100]{1,0:T(8,128)S(1)} %get-tuple-element.34), channel_id=1, source_target_pairs={{0,16},{1,17},{2,18},{3,19},{4,20},{5,21},{6,22},{7,23},{8,24},{9,... | collective-permute-start | bytes 38408 | tf_op jit(solution)/shard_map/ppermute | solution.py:39
  36.2 3.8 %collective-permute-start.8 = (f32[32,100]{1,0:T(8,128)S(1)}, f32[32,100]{1,0:T(8,128)S(1)}, u32[]{:S(2)}, u32[]{:S(2)}) collective-permute-start(f32[32,100]{1,0:T(8,128)S(1)} %add_add_fusion.1), channel_id=1, source_target_pairs={{0,4},{1,5},{2,6},{3,7},{4,0},{5,1},{6,2},{7,3},{8,12},{9,13},{10,... | collective-permute-start | bytes 38408 | tf_op jit(solution)/shard_map/ppermute | solution.py:39
  40.0 5.7 %collective-permute-start.11 = (f32[32,100]{1,0:T(8,128)S(1)}, f32[32,100]{1,0:T(8,128)S(1)}, u32[]{:S(2)}, u32[]{:S(2)}) collective-permute-start(f32[32,100]{1,0:T(8,128)S(1)} %add.36), channel_id=1, source_target_pairs={{0,2},{1,3},{2,0},{3,1},{4,6},{5,7},{6,4},{7,5},{8,10},{9,11},{10,... | collective-permute-start | bytes 38408 | tf_op jit(solution)/shard_map/ppermute | solution.py:39
  43.0 4.9 %collective-permute-start.10 = (f32[32,100]{1,0:T(8,128)S(1)}, f32[32,100]{1,0:T(8,128)S(1)}, u32[]{:S(2)}, u32[]{:S(2)}) collective-permute-start(f32[32,100]{1,0:T(8,128)S(1)} %add.36), channel_id=1, source_target_pairs={{0,3},{1,2},{2,1},{3,0},{4,7},{5,6},{6,5},{7,4},{8,11},{9,10},{10,... | collective-permute-start | bytes 38408 | tf_op jit(solution)/shard_map/ppermute | solution.py:39
  44.2 3.8 %collective-permute-start.9 = (f32[32,100]{1,0:T(8,128)S(1)}, f32[32,100]{1,0:T(8,128)S(1)}, u32[]{:S(2)}, u32[]{:S(2)}) collective-permute-start(f32[32,100]{1,0:T(8,128)S(1)} %add.36), channel_id=1, source_target_pairs={{0,1},{1,0},{2,3},{3,2},{4,5},{5,4},{6,7},{7,6},{8,9},{9,8},{10,11... | collective-permute-start | bytes 38408 | tf_op jit(solution)/shard_map/ppermute | solution.py:39
  51.4 1.3 %collective-permute-start.12 = (f32[3,8,1024]{2,1,0:T(8,128)S(1)}, f32[3,8,1024]{2,1,0:T(8,128)S(1)}, u32[]{:S(2)}, u32[]{:S(2)}) collective-permute-start(f32[3,8,1024]{2,1,0:T(8,128)S(1)} %get-tuple-element.51), channel_id=1, source_target_pairs={{0,8},{1,9},{2,10},{3,11},{4,12},{5,13},{6,14},{7,15},{8,0},{9,1},... | collective-permute-start | bytes 294920 | tf_op jit(solution)/shard_map/ppermute | solution.py:39
  52.7 5.7 %collective-permute-start.13 = (f32[3,4,1024]{2,1,0:T(4,128)S(1)}, f32[3,4,1024]{2,1,0:T(4,128)S(1)}, u32[]{:S(2)}, u32[]{:S(2)}) collective-permute-start(f32[3,4,1024]{2,1,0:T(4,128)S(1)} %slice.11), channel_id=1, source_target_pairs={{0,64},{1,65},{2,66},{3,67},{4,68},{5,69},{6,70},{7,71},{8,72},{9,... | collective-permute-start | bytes 147464 | tf_op jit(solution)/shard_map/ppermute | solution.py:39

commit v2 on v1

--- a/solution.py
+++ b/solution.py
@@ -105,6 +105,33 @@
     return jnp.concatenate([one, one], axis=0)
 
 
+def pick_kernel(
+    index_hbm, label_hbm, pool_hbm, dual_hbm, mine_hbm, block_ref, dual_ref, mine_ref, hot_ref,
+    index_ref, label_ref, pool_ref, index_sem, label_sem, pool_sem, dual_sem, mine_sem,
+):
+    copies = [
+        pltpu.make_async_copy(index_hbm, index_ref, index_sem),
+        pltpu.make_async_copy(pool_hbm, pool_ref, pool_sem),
+        pltpu.make_async_copy(label_hbm, label_ref, label_sem),
+        pltpu.make_async_copy(dual_hbm, dual_ref, dual_sem),
+        pltpu.make_async_copy(mine_hbm, mine_ref, mine_sem),
+    ]
+    for copy in copies:
+        copy.start()
+    for copy in copies:
+        copy.wait()
+    base = lax.axis_index("tgt") * pool_ref.shape[1]
+    for t in range(8):
+        one = pool_ref[:, pl.ds(index_ref[t] - base, 1), :]
+        for c in range(3):
+            block_ref[c * 8 + t : c * 8 + t + 1] = one[c]
+    row = lax.broadcasted_iota(jnp.int32, (8, CLASSES), 0)
+    own = jnp.zeros((8, CLASSES), jnp.int32)
+    for t in range(8):
+        own = jnp.where(row == t, label_ref[t], own)
+    hot_ref[...] = jnp.where(own == lax.broadcasted_iota(jnp.int32, (8, CLASSES), 1), 1.0, 0.0)
+
+
 def pixel_box(v):
     lane = lax.broadcasted_iota(jnp.int32, v.shape, 1)
     col = lane & (SIDE - 1)
@@ -114,7 +141,7 @@
     return v + above + below
 
 
-def spread_kernel(s_ref, y_ref, rb_ref, sb_ref, q_ref):
+def spread_kernel(s0_ref, s1_ref, s2_ref, s3_ref, y_ref, rb_ref, sb_ref, q_ref, parts_ref):
     def keep(k, v):
         for i in range(ROWS):
             row = jnp.concatenate([v[:, q * 256 + i * SIDE : q * 256 + (i + 1) * SIDE] for q in range(4)], axis=1)
@@ -123,7 +150,7 @@
 
     energy = None
     for c in range(3):
-        image = s_ref[c]
+        image = jnp.concatenate([ref[c] for ref in (s0_ref, s1_ref, s2_ref, s3_ref)], axis=0)
         energy = image * image if energy is None else energy + image * image
         keep(c, image * (1.0 / 27.0))
     level = pixel_box(energy * (1.0 / 27.0)) + BETA
@@ -134,30 +161,48 @@
             level = pixel_box(level * (1.0 / 9.0)) + BETA
 
     first = lax.broadcasted_iota(jnp.int32, (DEEP * SG, 128), 1) // TG * SIDE
-
-    def body(j, carry):
-        for k in range(6):
-            one = jnp.take_along_axis(q_ref[k], first + j, axis=1).reshape(1, DEEP, SG, 128)
-            if k < 3:
-                y_ref[k, pl.ds(j, 1)] = one
-            else:
-                rb_ref[k - 3, pl.ds(j, 1)] = one
-                sb_ref[k - 3, pl.ds(j, 1)] = lax.rsqrt(one * one) * (1.0 / 9.0)
-        return carry
-
-    lax.fori_loop(0, SIDE, body, 0, unroll=2)
+    image = q_ref[:3].reshape(3 * 128, 128)
+    hi = image.astype(jnp.bfloat16)
+    rest = image - hi.astype(F32)
+    mid = rest.astype(jnp.bfloat16)
+    low = (rest - mid.astype(F32)).astype(jnp.bfloat16)
+    parts_ref[...] = jnp.concatenate([hi, mid, low], axis=1)
+    row = lax.broadcasted_iota(jnp.int32, (128, 256), 0)
+    lane = lax.broadcasted_iota(jnp.int32, (128, 256), 1)
+    place = row - (lane & 127) // TG * SIDE - lax.shift_right_logical(lane, 7)
+
+    def body(k, carry):
+        pick = jnp.where(place == 2 * k, 1.0, 0.0).astype(jnp.bfloat16)
+        both = jnp.dot(parts_ref[...], jnp.concatenate([pick] * 3, axis=0), preferred_element_type=F32)
+        for n in range(2):
+            j = 2 * k + n
+            y_ref[:, pl.ds(j, 1)] = both[:, n * 128 : (n + 1) * 128].reshape(3, 1, DEEP, SG, 128)
+            for l in range(3):
+                one = jnp.take_along_axis(q_ref[3 + l], first + j, axis=1).reshape(1, DEEP, SG, 128)
+                rb_ref[l, pl.ds(j, 1)] = one
+                sb_ref[l, pl.ds(j, 1)] = lax.rsqrt(one * one) * (1.0 / 9.0)
+        return carry
+
+    lax.fori_loop(0, SIDE // 2, body, 0, unroll=4)
 
 
 def spread(ref, k, j):
     return ref[k, pl.ds(j, 1)][0]
 
 
-def own_duals(place_ref, dual_ref):
-    return [dual_ref[pl.ds(place_ref[4 + k] * 4, 4), :] for k in range(4)]
+def own_duals(dual_ref):
+    tgt = lax.axis_index("tgt")
+    return [dual_ref[pl.ds((tgt ^ k) * 4, 4), :] for k in (0, 1, 8, 9)]
+
+
+def block_rows(ref, r):
+    z = lax.axis_index("tgt") // 2 % 4
+    at_z = (z, z ^ 1, 3 - z, z ^ 2)[r]
+    return ref.at[pl.ds(pl.multiple_of(at_z * 8, 8), 8), :]
 
 
 def forward_kernel(
-    place_ref, x_ref, y_ref, rb_ref, sb_ref, dual_ref, label_ref,
+    x_ref, y_ref, rb_ref, sb_ref, dual_ref, hot_ref,
     pred_ref, xt_ref, h0_ref, h1_ref, w0_ref, w1_ref, w2_ref, v2_ref,
     ra_ref, sa_ref, va_ref, vb_ref,
 ):
@@ -231,7 +276,7 @@
     lax.fori_loop(0, SIDE // 2, layer1, 0, unroll=2)
     total = lax.fori_loop(0, SIDE // 2, layer2, jnp.zeros((2, SG, 128), F32), unroll=2)
     kernel = total * (9.0 / PIXELS)
-    duals = own_duals(place_ref, dual_ref)
+    duals = own_duals(dual_ref)
     wide_pred = None
     for g in range(2):
         part = lax.dot_general(
@@ -243,13 +288,8 @@
     for r in range(4):
         rows = pred[r * 8 : (r + 1) * 8]
         if r == 0:
-            row = lax.broadcasted_iota(jnp.int32, rows.shape, 0)
-            own = jnp.zeros(rows.shape, jnp.int32)
-            for t in range(8):
-                own = jnp.where(row == t, label_ref[t], own)
-            hot = (own == lax.broadcasted_iota(jnp.int32, rows.shape, 1)) & (place_ref[8] == 0)
-            rows = rows - jnp.where(hot, 1.0, 0.0)
-        pred_ref[pl.ds(pl.multiple_of(place_ref[r] * 8, 8), 8), :] = rows
+            rows = rows - jnp.where(lax.axis_index("sup") == 0, hot_ref[...], 0.0)
+        block_rows(pred_ref, r)[...] = rows
 
 
 def clear_edges(*refs):
@@ -308,11 +348,11 @@
     lax.fori_loop(0, SIDE // 2, body, 0)
 
 
-def sum_kernel(place_ref, res_ref, dual_ref, g_ref, own_ref, *out_refs):
-    own_ref[...] = res_ref[pl.ds(pl.multiple_of(place_ref[0] * 8, 8), 8), :]
-    rows = [res_ref[pl.ds(pl.multiple_of(place_ref[r] * 8, 8), 8), :] for r in range(4)]
+def sum_kernel(res_ref, dual_ref, g_ref, own_ref, *out_refs):
+    own_ref[...] = block_rows(res_ref, 0)[...]
+    rows = [block_rows(res_ref, r)[...] for r in range(4)]
     weight = lax.dot_general(
-        jnp.concatenate(own_duals(place_ref, dual_ref), axis=0) * (1.0 / 3.0), jnp.concatenate(rows * 4, axis=0), (((1,), (1,)), ((), ())),
+        jnp.concatenate(own_duals(dual_ref), axis=0) * (1.0 / 3.0), jnp.concatenate(rows * 4, axis=0), (((1,), (1,)), ((), ())),
         precision=lax.Precision.HIGHEST, preferred_element_type=F32,
     )
     weight = jnp.broadcast_to(weight.reshape(2, 1, SG, 128), (2, ROWS, SG, 128)).reshape(DEEP, SG, 128)
@@ -350,49 +390,54 @@
     return jax.ShapeDtypeStruct(shape, F32)
 
 
+def cost(mib):
+    return pl.CostEstimate(flops=0, transcendentals=0, bytes_accessed=mib << 20)
+
+
 def params(mib):
     return pltpu.CompilerParams(vmem_limit_bytes=mib << 20)
 
 
 def shards(target_pool, target_index, target_labels, dual_weights, support_images):
-    tgt = lax.axis_index("tgt")
-    sup = lax.axis_index("sup")
-    z = (tgt // 2) % 4
-
     mine = support_images.transpose(1, 0, 2)
-    pair = jnp.concatenate([mine, send(mine, other_core)], axis=1)
-    target_index, pair = lax.optimization_barrier((target_index, pair))
-    support = jnp.concatenate([pair, send(pair, other_y)], axis=1)
-    rows = (target_index - tgt * target_pool.shape[0]).astype(jnp.uint32)
-    targets = target_pool.at[rows].get(mode="promise_in_bounds")
-    block = targets.transpose(1, 0, 2).reshape(24, PIXELS)
+    across = send(mine, other_y)
+    beside = send(mine, other_core)
+    hbm = pl.BlockSpec(memory_space=pltpu.HBM)
+    dma = pltpu.SemaphoreType.DMA(())
+    pool = target_pool.transpose(1, 0, 2)
+    block, duals, here, hot = pl.pallas_call(
+        pick_kernel, out_shape=(vm(24, PIXELS), vm(*dual_weights.shape), vm(*mine.shape), vm(8, CLASSES)),
+        in_specs=[hbm] * 5, out_specs=(VMEM,) * 4,
+        scratch_shapes=[pltpu.SMEM((8,), jnp.int32), pltpu.SMEM((8,), jnp.int32), pltpu.VMEM(pool.shape, F32)] + [dma] * 5,
+        compiler_params=params(4), name="pick", cost_estimate=cost(2),
+    )(*[pltpu.with_memory_space_constraint(v, pltpu.HBM) for v in (target_index, target_labels, pool, dual_weights, mine)])
+    block, beside = lax.optimization_barrier((block, beside))
+    support = [here, beside, across, send(across, other_core)]
     x_all = jnp.stack([block, send(block, STEPS[0]), send(block, STEPS[1]), send(block, far_z)])
-    place = jnp.stack([z, z ^ 1, 3 - z, z ^ 2] + [tgt ^ k for k in (0, 1, 8, 9)] + [sup]).astype(jnp.int32)
-
     spread_shape = (3, SIDE, DEEP, SG, 128)
     y_wide, rb_wide, sb_wide = pl.pallas_call(
-        spread_kernel, out_shape=(vm(*spread_shape),) * 3, in_specs=[VMEM], out_specs=(VMEM,) * 3,
-        scratch_shapes=[pltpu.VMEM((6, DEEP * SG, 128), F32)], compiler_params=params(6), name="spread",
-    )(support)
+        spread_kernel, out_shape=(vm(*spread_shape),) * 3, in_specs=[VMEM] * 4, out_specs=(VMEM,) * 3,
+        scratch_shapes=[pltpu.VMEM((6, DEEP * SG, 128), F32), pltpu.VMEM((3 * 128, 3 * 128), jnp.bfloat16)], compiler_params=params(6), name="spread", cost_estimate=cost(12),
+    )(*support)
 
     column = (SIDE, DEEP, SG, 128)
     padded = (SIDE + 2, DEEP, SG, 128)
     flat = (3, ROWS, SIDE, 128)
 
-    def near_call(kernel, outs, ins, name, scratch=(), mib=6):
+    def near_call(kernel, outs, ins, name, moved, scratch=(), mib=6):
         return pl.pallas_call(
             kernel, out_shape=tuple(vm(*o) for o in outs), in_specs=[VMEM] * len(ins), out_specs=(VMEM,) * len(outs),
-            scratch_shapes=[pltpu.VMEM(v, F32) for v in scratch], compiler_params=params(mib), name=name,
+            scratch_shapes=[pltpu.VMEM(v, F32) for v in scratch], compiler_params=params(mib), name=name, cost_estimate=cost(moved),
         )(*map(near, ins))
 
     pred, xt, h0, h1, w0, w1, w2, v2 = pl.pallas_call(
         forward_kernel,
         out_shape=(hb(TG, CLASSES), vm(*flat), vm(*column), vm(*column), vm(*column), vm(*column), vm(*column), vm(*padded)),
-        in_specs=[SMEM] + [VMEM] * 5 + [SMEM],
+        in_specs=[VMEM] * 6,
         out_specs=(VMEM,) * 8,
         scratch_shapes=[pltpu.VMEM(flat, F32), pltpu.VMEM(flat, F32), pltpu.VMEM(padded, F32), pltpu.VMEM(padded, F32)],
-        compiler_params=params(14), name="forward",
-    )(place, x_all, near(y_wide), near(rb_wide), near(sb_wide), dual_weights, target_labels)
+        compiler_params=params(14), name="forward", cost_estimate=cost(32),
+    )(x_all, near(y_wide), near(rb_wide), near(sb_wide), near(duals), near(hot))
 
     def around(res, moves):
         near_a, near_b, far = [send(res, move) for move in moves]
@@ -401,22 +446,22 @@
     res, v2 = lax.optimization_barrier((pred, v2))
     added = around(res, (STEPS[0], STEPS[1], far_z))
     v0, l0, p1 = near_call(
-        back_kernel_a, (padded, column, padded), (v2, h1, w1, w2, h0, w0, rb_wide), "back_a",
+        back_kernel_a, (padded, column, padded), (v2, h1, w1, w2, h0, w0, rb_wide), "back_a", 8,
         scratch=(column, padded, padded), mib=9,
     )
     res, l0 = lax.optimization_barrier((added(), l0))
     new = send(res, STEPS[2])
-    (p0,) = near_call(back_kernel_b, (padded,), (l0, p1), "back_b")
+    (p0,) = near_call(back_kernel_b, (padded,), (l0, p1), "back_b", 3)
     res, p0 = lax.optimization_barrier((res + new, p0))
     added = around(res, (STEPS[3], STEPS[4], far_x))
-    (g,) = near_call(back_kernel_c, ((3,) + column,), (v0, p0, xt, y_wide), "back_c")
+    (g,) = near_call(back_kernel_c, ((3,) + column,), (v0, p0, xt, y_wide), "back_c", 5)
     res = added()
 
     residual, *parts = pl.pallas_call(
         sum_kernel, out_shape=(hb(8, CLASSES),) + (hb(3, 8, PIXELS),) * 2,
-        in_specs=[SMEM] + [VMEM] * 3, out_specs=(VMEM,) * 3,
-        compiler_params=params(10), name="weighted",
-    )(place, res, dual_weights, near(g))
+        in_specs=[VMEM] * 3, out_specs=(VMEM,) * 3,
+        compiler_params=params(10), name="weighted", cost_estimate=cost(10),
+    )(res, near(duals), near(g))
     pair = parts[0] + send(parts[1], other_core)
     total = pair[:, :4] + send(pair[:, 4:], other_y)
     return (residual, total.transpose(1, 0, 2))

time: 59.2 us -> 54.7 us (0.924)
  Pallas kernels: 22.4 us -> 20.5 us
  other arithmetic: 2.2 us -> 0.69 us
  local copies, waits for them, and re-layouts: 0.81 us -> 0.01 us
    pallas_call x1, Pallas kernels: 5.5 us -> 3.27 us  [shards(): pl.pallas_call(spread_kernel, out_shape=(vm(*spread_shape),) * 3, in_spec...]
    pallas_call x0 -> x1, Pallas kernels: none -> 1.23 us  [shards(): pl.pallas_call(pick_kernel, out_shape=(vm(24, PIXELS), vm(*dual_weights.s...]
    concatenate x2 -> x0, other arithmetic: 0.84 us -> none  [the longest x1 0.82 us: shards(): pair = jnp.concatenate([mine, send(mine, other_core)], axis=1)]
    gather x1 -> x0, local copies, waits for them, and re-layouts: 0.69 us -> none  [shards(): targets = target_pool.at[rows].get(mode='promise_in_bounds')]
    convert_element_type x1 -> x0, other arithmetic: 0.66 us -> none  [shards(): targets = target_pool.at[rows].get(mode='promise_in_bounds')]
    ppermute x14 -> x15, starting transfers between devices: 18.4 us -> 18 us  [send(): return lax.ppermute(x, AXES, pairs_of(move))]
    ppermute x14 -> x15, waiting for transfers between devices: 14.4 us -> 14.7 us  [send(): return lax.ppermute(x, AXES, pairs_of(move))]
  transfers between devices with their start and end apart: 14 -> 15, of which waited for: 6 -> 8; matrix products, arithmetic and copies ran while one was open for 2% -> 0% of each run, Pallas kernels for 17% -> 16%
where the time goes in v2:
time: 54.7 us; the launch traced here: 54.6 us
  Pallas kernels  20.5 us (37%)
  starting transfers between devices  18 us (33%)
  waiting for transfers between devices  14.7 us (27%)
  between operations  0.73 us (1%)
  other arithmetic  0.69 us (1%)
    ppermute x15, starting transfers between devices, send(): return lax.ppermute(x, AXES, pairs_of(move))  18 us
    ppermute x15, waiting for transfers between devices, send(): return lax.ppermute(x, AXES, pairs_of(move))  14.7 us
    pallas_call x1, Pallas kernels, shards(): pl.pallas_call(forward_kernel, out_shape=(hb(TG, CLASSES), vm(*flat), vm(...  8.65 us
    pallas_call x3, Pallas kernels, near_call(): pl.pallas_call(kernel, out_shape=tuple((vm(*o) for o in outs)), in_specs=...  4.48 us
    pallas_call x1, Pallas kernels, shards(): pl.pallas_call(spread_kernel, out_shape=(vm(*spread_shape),) * 3, in_spec...  3.27 us
    pallas_call x1, Pallas kernels, shards(): pl.pallas_call(sum_kernel, out_shape=(hb(8, CLASSES),) + (hb(3, 8, PIXELS...  2.86 us
    pallas_call x1, Pallas kernels, shards(): pl.pallas_call(pick_kernel, out_shape=(vm(24, PIXELS), vm(*dual_weights.s...  1.23 us
  transfers between devices with their start and end apart: 15, of which 8 were waited for; matrix products, arithmetic and copies ran while one was open for 0% of the time, Pallas kernels for 16%

profile of v2, /device:TPU:0, one launch (start us, length us, event | category | flops | bytes accessed | tf_op | source)
XLA Modules:
  0.0 54.6 jit_solution(3153380821604781204)
XLA Ops:
  0.7 3.4 %collective-permute-start.4 = (f32[3,4,1024]{2,1,0:T(4,128)}, f32[3,4,1024]{2,1,0:T(4,128)S(1)}, u32[]{:S(2)}, u32[]{:S(2)}) collective-permute-start(f32[3,4,1024]{2,1,0:T(4,128)} %bitcast.14), channel_id=1, source_target_pairs={{0,64},{1,65},{2,66},{3,67},{4,68},{5,69},{6,70},{7,71},{8,72},{9,... | collective-permute-start | bytes 147464 | tf_op jit(solution)/shard_map/ppermute | solution.py:39
  4.1 1.2 %pick.1 = (f32[24,1024]{1,0:T(8,128)S(1)}, f32[64,100]{1,0:T(8,128)S(1)}, f32[3,4,1024]{2,1,0:T(4,128)S(1)}, f32[8,100]{1,0:T(8,128)S(1)}) custom-call(s32[8]{0:T(128)} %index_hbm.1, s32[8]{0:T(128)} %label_hbm.1, f32[3,64,1024]{2,1,0:T(8,128)} %bitcast.9, f32[64,100]{1,0:T(8,128)} %dual_hbm.1, f32[3,4,1024]{2,1,0:T(4,128)} %bitcast.15), custom_call_target="tpu_custom_call" | custom-call | bytes 2097152 | tf_op jit(solution)/shard_map/pick/pallas_call | solution.py:408
  5.3 4.0 %collective-permute-start.3 = (f32[24,1024]{1,0:T(8,128)S(1)}, f32[24,1024]{1,0:T(8,128)S(1)}, u32[]{:S(2)}, u32[]{:S(2)}) collective-permute-start(f32[24,1024]{1,0:T(8,128)S(1)} %get-tuple-element.32), channel_id=1, source_target_pairs={{0,32},{1,33},{2,34},{3,35},{4,36},{5,37},{6,38},{7,39},{8,40},{9,... | collective-permute-start | bytes 294920 | tf_op jit(solution)/shard_map/ppermute | solution.py:39
  9.3 0.7 %collective-permute-start.2 = (f32[24,1024]{1,0:T(8,128)S(1)}, f32[24,1024]{1,0:T(8,128)S(1)}, u32[]{:S(2)}, u32[]{:S(2)}) collective-permute-start(f32[24,1024]{1,0:T(8,128)S(1)} %get-tuple-element.32), channel_id=1, source_target_pairs={{0,48},{1,49},{2,50},{3,51},{4,52},{5,53},{6,54},{7,55},{8,56},{9,... | collective-permute-start | bytes 294920 | tf_op jit(solution)/shard_map/ppermute | solution.py:39
  10.0 0.3 collective-permute-start.1
  10.3 1.2 %collective-permute-done.5.s3_ref = f32[3,4,1024]{2,1,0:T(4,128)S(1)} collective-permute-done((f32[3,4,1024]{2,1,0:T(4,128)S(1)}, f32[3,4,1024]{2,1,0:T(4,128)S(1)}, u32[]{:S(2)}, u32[]{:S(2)}) %collective-permute-start.5) | collective-permute-done | bytes 49184 | tf_op jit(solution)/shard_map/ppermute | solution.py:39
  11.5 3.3 %spread.1 = (f32[3,32,16,8,128]{4,3,2,1,0:T(8,128)S(1)}, f32[3,32,16,8,128]{4,3,2,1,0:T(8,128)S(1)}, f32[3,32,16,8,128]{4,3,2,1,0:T(8,128)S(1)}) custom-call(f32[3,4,1024]{2,1,0:T(4,128)S(1)} %get-tuple-element.33.s0_ref, f32[3,4,1024]{2,1,0:T(4,128)S(1)} %collective-permute-done.s1_ref, f32[3,4,1024]{2,1,0:T(4,128)S(1)} %collective-permute-done.4.s2_ref, ...), custom_call_target="tpu_custom_call" | custom-call | bytes 12582912 | tf_op jit(solution)/shard_map/spread/pallas_call | solution.py:418
  15.3 8.7 %forward.1 = (f32[32,100]{1,0:T(8,128)S(1)}, f32[3,8,32,128]{3,2,1,0:T(8,128)S(1)}, f32[32,16,8,128]{3,2,1,0:T(8,128)S(1)}, f32[32,16,8,128]{3,2,1,0:T(8,128)S(1...) custom-call(f32[4,24,1024]{2,1,0:T(8,128)S(1)} %pad_maximum_fusion.x, ...), custom_call_target="tpu_custom_call" | custom-call | bytes 33554432 | tf_op jit(solution)/shard_map/forward/pallas_call | solution.py:433
  24.0 3.3 %collective-permute-start.8 = (f32[32,100]{1,0:T(8,128)S(1)}, f32[32,100]{1,0:T(8,128)S(1)}, u32[]{:S(2)}, u32[]{:S(2)}) collective-permute-start(f32[32,100]{1,0:T(8,128)S(1)} %get-tuple-element.42), channel_id=1, source_target_pairs={{0,32},{1,33},{2,34},{3,35},{4,36},{5,37},{6,38},{7,39},{8,40},{9,... | collective-permute-start | bytes 38408 | tf_op jit(solution)/shard_map/ppermute | solution.py:39
  27.3 0.7 %collective-permute-start.7 = (f32[32,100]{1,0:T(8,128)S(1)}, f32[32,100]{1,0:T(8,128)S(1)}, u32[]{:S(2)}, u32[]{:S(2)}) collective-permute-start(f32[32,100]{1,0:T(8,128)S(1)} %get-tuple-element.42), channel_id=1, source_target_pairs={{0,48},{1,49},{2,50},{3,51},{4,52},{5,53},{6,54},{7,55},{8,56},{9,... | collective-permute-start | bytes 38408 | tf_op jit(solution)/shard_map/ppermute | solution.py:39
  28.0 2.2 %back_a.1 = (f32[34,16,8,128]{3,2,1,0:T(8,128)S(1)}, f32[32,16,8,128]{3,2,1,0:T(8,128)S(1)}, f32[34,16,8,128]{3,2,1,0:T(8,128)S(1)}) custom-call(f32[34,16,8,128]{3,2,1,0:T(8,128)S(1)} %get-tuple-element.43.v2_ref, f32[32,16,8,128]{3,2,1,0:T(8,128)S(1)} %get-tuple-element.44.h1_ref, f32[32,16,8,128]{3,2,1,0:T(8,128)S(1)} %get-tuple-element.45.w1_ref, ...), custom_call_target="tpu_custom_call" | custom-call | bytes 8388608 | tf_op jit(solution)/shard_map/back_a/pallas_call | solution.py:428
  30.2 2.0 %collective-permute-done.7 = f32[32,100]{1,0:T(8,128)S(1)} collective-permute-done((f32[32,100]{1,0:T(8,128)S(1)}, f32[32,100]{1,0:T(8,128)S(1)}, u32[]{:S(2)}, u32[]{:S(2)}) %collective-permute-start.7) | collective-permute-done | bytes 12832 | tf_op jit(solution)/shard_map/ppermute | solution.py:39
  32.3 0.8 %collective-permute-start.9 = (f32[32,100]{1,0:T(8,128)S(1)}, f32[32,100]{1,0:T(8,128)S(1)}, u32[]{:S(2)}, u32[]{:S(2)}) collective-permute-start(f32[32,100]{1,0:T(8,128)S(1)} %add_add_fusion.1), channel_id=1, source_target_pairs={{0,4},{1,5},{2,6},{3,7},{4,0},{5,1},{6,2},{7,3},{8,12},{9,13},{10,... | collective-permute-start | bytes 38408 | tf_op jit(solution)/shard_map/ppermute | solution.py:39
  33.0 0.7 %back_b.1.p0_ref = f32[34,16,8,128]{3,2,1,0:T(8,128)S(1)} custom-call(f32[32,16,8,128]{3,2,1,0:T(8,128)S(1)} %get-tuple-element.51.l0_ref, f32[34,16,8,128]{3,2,1,0:T(8,128)S(1)} %get-tuple-element.52.p1_ref), custom_call_target="tpu_custom_call" | custom-call | bytes 3145728 | tf_op jit(solution)/shard_map/back_b/pallas_call | solution.py:428
  33.8 2.3 %collective-permute-done.9 = f32[32,100]{1,0:T(8,128)S(1)} collective-permute-done((f32[32,100]{1,0:T(8,128)S(1)}, f32[32,100]{1,0:T(8,128)S(1)}, u32[]{:S(2)}, u32[]{:S(2)}) %collective-permute-start.9) | collective-permute-done | bytes 12832 | tf_op jit(solution)/shard_map/ppermute | solution.py:39
  36.1 3.0 %collective-permute-start.12 = (f32[32,100]{1,0:T(8,128)S(1)}, f32[32,100]{1,0:T(8,128)S(1)}, u32[]{:S(2)}, u32[]{:S(2)}) collective-permute-start(f32[32,100]{1,0:T(8,128)S(1)} %add.30), channel_id=1, source_target_pairs={{0,2},{1,3},{2,0},{3,1},{4,6},{5,7},{6,4},{7,5},{8,10},{9,11},{10,... | collective-permute-start | bytes 38408 | tf_op jit(solution)/shard_map/ppermute | solution.py:39
  39.1 1.1 %collective-permute-start.11 = (f32[32,100]{1,0:T(8,128)S(1)}, f32[32,100]{1,0:T(8,128)S(1)}, u32[]{:S(2)}, u32[]{:S(2)}) collective-permute-start(f32[32,100]{1,0:T(8,128)S(1)} %add.30), channel_id=1, source_target_pairs={{0,3},{1,2},{2,1},{3,0},{4,7},{5,6},{6,5},{7,4},{8,11},{9,10},{10,... | collective-permute-start | bytes 38408 | tf_op jit(solution)/shard_map/ppermute | solution.py:39
  40.3 1.6 %back_c.1.g_ref = f32[3,32,16,8,128]{4,3,2,1,0:T(8,128)S(1)} custom-call(f32[34,16,8,128]{3,2,1,0:T(8,128)S(1)} %get-tuple-element.54.v0_ref, f32[34,16,8,128]{3,2,1,0:T(8,128)S(1)} %back_b.1.p0_ref, f32[3,8,32,128]{3,2,1,0:T(8,128)S(1)} %get-tuple-element.56.xt_ref, f32[3,32,16,8,128]{4,3,2,1,0:T(8,128)S(1)} %get-tuple-element.35.y_ref), custom_call_target="tpu_custom_call" | custom-call | bytes 5242880 | tf_op jit(solution)/shard_map/back_c/pallas_call | solution.py:428
  41.8 2.2 %collective-permute-done.11 = f32[32,100]{1,0:T(8,128)S(1)} collective-permute-done((f32[32,100]{1,0:T(8,128)S(1)}, f32[32,100]{1,0:T(8,128)S(1)}, u32[]{:S(2)}, u32[]{:S(2)}) %collective-permute-start.11) | collective-permute-done | bytes 12832 | tf_op jit(solution)/shard_map/ppermute | solution.py:39
  44.1 2.9 %weighted.1 = (f32[8,100]{1,0:T(8,128)}, f32[3,8,1024]{2,1,0:T(8,128)S(1)}, f32[3,8,1024]{2,1,0:T(8,128)S(1)}) custom-call(f32[32,100]{1,0:T(8,128)S(1)} %add_add_fusion.res_ref, f32[64,100]{1,0:T(8,128)S(1)} %get-tuple-element.38.dual_ref, f32[3,32,16,8,128]{4,3,2,1,0:T(8,128)S(1)} %back_c.1.g_ref), custom_call_target="tpu_custom_call" | custom-call | bytes 10485760 | tf_op jit(solution)/shard_map/weighted/pallas_call | solution.py:460
  46.9 1.3 %collective-permute-done.13 = f32[3,8,1024]{2,1,0:T(8,128)S(1)} collective-permute-done((f32[3,8,1024]{2,1,0:T(8,128)S(1)}, f32[3,8,1024]{2,1,0:T(8,128)S(1)}, u32[]{:S(2)}, u32[]{:S(2)}) %collective-permute-start.13) | collective-permute-done | bytes 98336 | tf_op jit(solution)/shard_map/ppermute | solution.py:39
  48.3 0.6 %collective-permute-start.14 = (f32[3,4,1024]{2,1,0:T(4,128)S(1)}, f32[3,4,1024]{2,1,0:T(4,128)S(1)}, u32[]{:S(2)}, u32[]{:S(2)}) collective-permute-start(f32[3,4,1024]{2,1,0:T(4,128)S(1)} %slice.9), channel_id=1, source_target_pairs={{0,64},{1,65},{2,66},{3,67},{4,68},{5,69},{6,70},{7,71},{8,72},{9,... | collective-permute-start | bytes 147464 | tf_op jit(solution)/shard_map/ppermute | solution.py:39
  48.9 5.1 %collective-permute-done.14 = f32[3,4,1024]{2,1,0:T(4,128)S(1)} collective-permute-done((f32[3,4,1024]{2,1,0:T(4,128)S(1)}, f32[3,4,1024]{2,1,0:T(4,128)S(1)}, u32[]{:S(2)}, u32[]{:S(2)}) %collective-permute-start.14) | collective-permute-done | bytes 49184 | tf_op jit(solution)/shard_map/ppermute | solution.py:39
  53.9 0.6 %fusion = f32[4,3,1024]{2,0,1:T(4,128)} fusion(f32[3,4,1024]{2,1,0:T(4,128)S(1)} %collective-permute-done.14, f32[3,8,1024]{2,1,0:T(8,128)S(1)} %add.34), kind=kLoop, calls=%fused_computation.2 | loop fusion | flops 12288 | bytes 147456 | tf_op jit(solution)/shard_map/transpose | solution.py:467
  (20 shorter events, 0.6 us)
Async XLA Ops:
  0.6 4.7 %collective-permute-start = (f32[3,4,1024]{2,1,0:T(4,128)}, f32[3,4,1024]{2,1,0:T(4,128)S(1)}, u32[]{:S(2)}, u32[]{:S(2)}) collective-permute-start(f32[3,4,1024]{2,1,0:T(4,128)} %bitcast.13), channel_id=1, source_target_pairs={{0,8},{1,9},{2,10},{3,11},{4,12},{5,13},{6,14},{7,15},{8,0},{9,1},... | collective-permute-start | bytes 147464 | tf_op jit(solution)/shard_map/ppermute | solution.py:39
  0.7 9.6 %collective-permute-start.4 = (f32[3,4,1024]{2,1,0:T(4,128)}, f32[3,4,1024]{2,1,0:T(4,128)S(1)}, u32[]{:S(2)}, u32[]{:S(2)}) collective-permute-start(f32[3,4,1024]{2,1,0:T(4,128)} %bitcast.14), channel_id=1, source_target_pairs={{0,64},{1,65},{2,66},{3,67},{4,68},{5,69},{6,70},{7,71},{8,72},{9,... | collective-permute-start | bytes 147464 | tf_op jit(solution)/shard_map/ppermute | solution.py:39
  5.3 9.5 %collective-permute-start.3 = (f32[24,1024]{1,0:T(8,128)S(1)}, f32[24,1024]{1,0:T(8,128)S(1)}, u32[]{:S(2)}, u32[]{:S(2)}) collective-permute-start(f32[24,1024]{1,0:T(8,128)S(1)} %get-tuple-element.32), channel_id=1, source_target_pairs={{0,32},{1,33},{2,34},{3,35},{4,36},{5,37},{6,38},{7,39},{8,40},{9,... | collective-permute-start | bytes 294920 | tf_op jit(solution)/shard_map/ppermute | solution.py:39
  9.3 5.8 %collective-permute-start.2 = (f32[24,1024]{1,0:T(8,128)S(1)}, f32[24,1024]{1,0:T(8,128)S(1)}, u32[]{:S(2)}, u32[]{:S(2)}) collective-permute-start(f32[24,1024]{1,0:T(8,128)S(1)} %get-tuple-element.32), channel_id=1, source_target_pairs={{0,48},{1,49},{2,50},{3,51},{4,52},{5,53},{6,54},{7,55},{8,56},{9,... | collective-permute-start | bytes 294920 | tf_op jit(solution)/shard_map/ppermute | solution.py:39
  10.0 5.3 %collective-permute-start.1 = (f32[24,1024]{1,0:T(8,128)S(1)}, f32[24,1024]{1,0:T(8,128)S(1)}, u32[]{:S(2)}, u32[]{:S(2)}) collective-permute-start(f32[24,1024]{1,0:T(8,128)S(1)} %get-tuple-element.32), channel_id=1, source_target_pairs={{0,16},{1,17},{2,18},{3,19},{4,20},{5,21},{6,22},{7,23},{8,24},{9,... | collective-permute-start | bytes 294920 | tf_op jit(solution)/shard_map/ppermute | solution.py:39
  10.3 1.2 %collective-permute-start.5 = (f32[3,4,1024]{2,1,0:T(4,128)S(1)}, f32[3,4,1024]{2,1,0:T(4,128)S(1)}, u32[]{:S(2)}, u32[]{:S(2)}) collective-permute-start(f32[3,4,1024]{2,1,0:T(4,128)S(1)} %collective-permute-done.4.s2_ref), channel_id=1, source_target_pairs={{0,8},{1,9},{2,10},{3,11},{4,12},{5,13},{6,14},{7,15},{8,0},{9,1},... | collective-permute-start | bytes 147464 | tf_op jit(solution)/shard_map/ppermute | solution.py:39
  24.0 6.2 %collective-permute-start.8 = (f32[32,100]{1,0:T(8,128)S(1)}, f32[32,100]{1,0:T(8,128)S(1)}, u32[]{:S(2)}, u32[]{:S(2)}) collective-permute-start(f32[32,100]{1,0:T(8,128)S(1)} %get-tuple-element.42), channel_id=1, source_target_pairs={{0,32},{1,33},{2,34},{3,35},{4,36},{5,37},{6,38},{7,39},{8,40},{9,... | collective-permute-start | bytes 38408 | tf_op jit(solution)/shard_map/ppermute | solution.py:39
  27.3 4.9 %collective-permute-start.7 = (f32[32,100]{1,0:T(8,128)S(1)}, f32[32,100]{1,0:T(8,128)S(1)}, u32[]{:S(2)}, u32[]{:S(2)}) collective-permute-start(f32[32,100]{1,0:T(8,128)S(1)} %get-tuple-element.42), channel_id=1, source_target_pairs={{0,48},{1,49},{2,50},{3,51},{4,52},{5,53},{6,54},{7,55},{8,56},{9,... | collective-permute-start | bytes 38408 | tf_op jit(solution)/shard_map/ppermute | solution.py:39
  28.0 4.2 %collective-permute-start.6 = (f32[32,100]{1,0:T(8,128)S(1)}, f32[32,100]{1,0:T(8,128)S(1)}, u32[]{:S(2)}, u32[]{:S(2)}) collective-permute-start(f32[32,100]{1,0:T(8,128)S(1)} %get-tuple-element.42), channel_id=1, source_target_pairs={{0,16},{1,17},{2,18},{3,19},{4,20},{5,21},{6,22},{7,23},{8,24},{9,... | collective-permute-start | bytes 38408 | tf_op jit(solution)/shard_map/ppermute | solution.py:39
  32.3 3.8 %collective-permute-start.9 = (f32[32,100]{1,0:T(8,128)S(1)}, f32[32,100]{1,0:T(8,128)S(1)}, u32[]{:S(2)}, u32[]{:S(2)}) collective-permute-start(f32[32,100]{1,0:T(8,128)S(1)} %add_add_fusion.1), channel_id=1, source_target_pairs={{0,4},{1,5},{2,6},{3,7},{4,0},{5,1},{6,2},{7,3},{8,12},{9,13},{10,... | collective-permute-start | bytes 38408 | tf_op jit(solution)/shard_map/ppermute | solution.py:39
  36.1 5.7 %collective-permute-start.12 = (f32[32,100]{1,0:T(8,128)S(1)}, f32[32,100]{1,0:T(8,128)S(1)}, u32[]{:S(2)}, u32[]{:S(2)}) collective-permute-start(f32[32,100]{1,0:T(8,128)S(1)} %add.30), channel_id=1, source_target_pairs={{0,2},{1,3},{2,0},{3,1},{4,6},{5,7},{6,4},{7,5},{8,10},{9,11},{10,... | collective-permute-start | bytes 38408 | tf_op jit(solution)/shard_map/ppermute | solution.py:39
  39.1 4.9 %collective-permute-start.11 = (f32[32,100]{1,0:T(8,128)S(1)}, f32[32,100]{1,0:T(8,128)S(1)}, u32[]{:S(2)}, u32[]{:S(2)}) collective-permute-start(f32[32,100]{1,0:T(8,128)S(1)} %add.30), channel_id=1, source_target_pairs={{0,3},{1,2},{2,1},{3,0},{4,7},{5,6},{6,5},{7,4},{8,11},{9,10},{10,... | collective-permute-start | bytes 38408 | tf_op jit(solution)/shard_map/ppermute | solution.py:39
  40.2 3.8 %collective-permute-start.10 = (f32[32,100]{1,0:T(8,128)S(1)}, f32[32,100]{1,0:T(8,128)S(1)}, u32[]{:S(2)}, u32[]{:S(2)}) collective-permute-start(f32[32,100]{1,0:T(8,128)S(1)} %add.30), channel_id=1, source_target_pairs={{0,1},{1,0},{2,3},{3,2},{4,5},{5,4},{6,7},{7,6},{8,9},{9,8},{10,11... | collective-permute-start | bytes 38408 | tf_op jit(solution)/shard_map/ppermute | solution.py:39
  46.9 1.3 %collective-permute-start.13 = (f32[3,8,1024]{2,1,0:T(8,128)S(1)}, f32[3,8,1024]{2,1,0:T(8,128)S(1)}, u32[]{:S(2)}, u32[]{:S(2)}) collective-permute-start(f32[3,8,1024]{2,1,0:T(8,128)S(1)} %get-tuple-element.59), channel_id=1, source_target_pairs={{0,8},{1,9},{2,10},{3,11},{4,12},{5,13},{6,14},{7,15},{8,0},{9,1},... | collective-permute-start | bytes 294920 | tf_op jit(solution)/shard_map/ppermute | solution.py:39
  48.3 5.7 %collective-permute-start.14 = (f32[3,4,1024]{2,1,0:T(4,128)S(1)}, f32[3,4,1024]{2,1,0:T(4,128)S(1)}, u32[]{:S(2)}, u32[]{:S(2)}) collective-permute-start(f32[3,4,1024]{2,1,0:T(4,128)S(1)} %slice.9), channel_id=1, source_target_pairs={{0,64},{1,65},{2,66},{3,67},{4,68},{5,69},{6,70},{7,71},{8,72},{9,... | collective-permute-start | bytes 147464 | tf_op jit(solution)/shard_map/ppermute | solution.py:39

commit v3 on v2

--- a/solution.py
+++ b/solution.py
@@ -302,8 +302,8 @@
     return ref[pl.ds(j, 1)][0]
 
 
-def back_kernel_a(v2_ref, h1_ref, w1_ref, w2_ref, h0_ref, w0_ref, rb_ref, v0_ref, l0_ref, p1_ref, l1_ref, v1_ref, p2_ref):
-    clear_edges(v1_ref, p2_ref, v0_ref, p1_ref)
+def back_kernel_a(v2_ref, h1_ref, w1_ref, w2_ref, rb_ref, l1_ref, v1_ref, p2_ref):
+    clear_edges(v1_ref, p2_ref)
 
     def layer1(k, carry):
         for j, up in columns(v2_ref, k):
@@ -314,6 +314,12 @@
             p2_ref[pl.ds(j + 1, 1)] = down(at(w2_ref, j) * (rb * rb))[None]
         return carry
 
+    lax.fori_loop(0, SIDE // 2, layer1, 0, unroll=2)
+
+
+def back_kernel_b(v1_ref, h0_ref, w0_ref, l1_ref, p2_ref, rb_ref, v0_ref, p0_ref, l0_ref, p1_ref):
+    clear_edges(v0_ref, p1_ref, p0_ref)
+
     def layer0(k, carry):
         for (j, up), (_, sums) in zip(columns(v1_ref, k), columns(p2_ref, k)):
             rb = spread(rb_ref, 0, j)
@@ -322,19 +328,13 @@
             p1_ref[pl.ds(j + 1, 1)] = down(at(l1_ref, j) + sums * (1.0 / 9.0))[None]
         return carry
 
-    lax.fori_loop(0, SIDE // 2, layer1, 0, unroll=2)
-    lax.fori_loop(0, SIDE // 2, layer0, 0, unroll=2)
-
-
-def back_kernel_b(l0_ref, p1_ref, p0_ref):
-    clear_edges(p0_ref)
-
-    def body(k, carry):
+    def last(k, carry):
         for j, sums in columns(p1_ref, k):
             p0_ref[pl.ds(j + 1, 1)] = down(at(l0_ref, j) + sums * (1.0 / 9.0))[None]
         return carry
 
-    lax.fori_loop(0, SIDE // 2, body, 0, unroll=2)
+    lax.fori_loop(0, SIDE // 2, layer0, 0, unroll=2)
+    lax.fori_loop(0, SIDE // 2, last, 0, unroll=2)
 
 
 def back_kernel_c(v0_ref, p0_ref, xt_ref, y_ref, g_ref):
@@ -445,13 +445,13 @@
 
     res, v2 = lax.optimization_barrier((pred, v2))
     added = around(res, (STEPS[0], STEPS[1], far_z))
-    v0, l0, p1 = near_call(
-        back_kernel_a, (padded, column, padded), (v2, h1, w1, w2, h0, w0, rb_wide), "back_a", 8,
-        scratch=(column, padded, padded), mib=9,
+    l1, v1, p2 = near_call(back_kernel_a, (column, padded, padded), (v2, h1, w1, w2, rb_wide), "back_a", 5)
+    res, v1 = lax.optimization_barrier((added(), v1))
+    new = send(res, STEPS[2])
+    v0, p0 = near_call(
+        back_kernel_b, (padded, padded), (v1, h0, w0, l1, p2, rb_wide), "back_b", 6,
+        scratch=(column, padded), mib=7,
     )
-    res, l0 = lax.optimization_barrier((added(), l0))
-    new = send(res, STEPS[2])
-    (p0,) = near_call(back_kernel_b, (padded,), (l0, p1), "back_b", 3)
     res, p0 = lax.optimization_barrier((res + new, p0))
     added = around(res, (STEPS[3], STEPS[4], far_x))
     (g,) = near_call(back_kernel_c, ((3,) + column,), (v0, p0, xt, y_wide), "back_c", 5)

time: 54.7 us -> 54.7 us (level)
  waiting for transfers between devices: 14.7 us -> 14.1 us
  transfers between devices with their start and end apart: 15 -> 15, of which waited for: 8 -> 9; matrix products, arithmetic and copies ran while one was open for 0% -> 0% of each run, Pallas kernels for 16% -> 17%
where the time goes in v3:
time: 54.7 us; the launch traced here: 54.6 us
  Pallas kernels  20.6 us (38%)
  starting transfers between devices  18.4 us (34%)
  waiting for transfers between devices  14.1 us (26%)
  between operations  0.72 us (1%)
  other arithmetic  0.69 us (1%)
    ppermute x15, starting transfers between devices, send(): return lax.ppermute(x, AXES, pairs_of(move))  18.4 us
    ppermute x15, waiting for transfers between devices, send(): return lax.ppermute(x, AXES, pairs_of(move))  14.1 us
    pallas_call x1, Pallas kernels, shards(): pl.pallas_call(forward_kernel, out_shape=(hb(TG, CLASSES), vm(*flat), vm(...  8.65 us
    pallas_call x3, Pallas kernels, near_call(): pl.pallas_call(kernel, out_shape=tuple((vm(*o) for o in outs)), in_specs=...  4.59 us
    pallas_call x1, Pallas kernels, shards(): pl.pallas_call(spread_kernel, out_shape=(vm(*spread_shape),) * 3, in_spec...  3.27 us
    pallas_call x1, Pallas kernels, shards(): pl.pallas_call(sum_kernel, out_shape=(hb(8, CLASSES),) + (hb(3, 8, PIXELS...  2.86 us
    pallas_call x1, Pallas kernels, shards(): pl.pallas_call(pick_kernel, out_shape=(vm(24, PIXELS), vm(*dual_weights.s...  1.23 us
  transfers between devices with their start and end apart: 15, of which 9 were waited for; matrix products, arithmetic and copies ran while one was open for 0% of the time, Pallas kernels for 17%

profile of v3, /device:TPU:0, one launch (start us, length us, event | category | flops | bytes accessed | tf_op | source)
XLA Modules:
  0.0 54.6 jit_solution(8157590403903288071)
XLA Ops:
  0.7 3.4 %collective-permute-start.4 = (f32[3,4,1024]{2,1,0:T(4,128)}, f32[3,4,1024]{2,1,0:T(4,128)S(1)}, u32[]{:S(2)}, u32[]{:S(2)}) collective-permute-start(f32[3,4,1024]{2,1,0:T(4,128)} %bitcast.14), channel_id=1, source_target_pairs={{0,64},{1,65},{2,66},{3,67},{4,68},{5,69},{6,70},{7,71},{8,72},{9,... | collective-permute-start | bytes 147464 | tf_op jit(solution)/shard_map/ppermute | solution.py:39
  4.1 1.2 %pick.1 = (f32[24,1024]{1,0:T(8,128)S(1)}, f32[64,100]{1,0:T(8,128)S(1)}, f32[3,4,1024]{2,1,0:T(4,128)S(1)}, f32[8,100]{1,0:T(8,128)S(1)}) custom-call(s32[8]{0:T(128)} %index_hbm.1, s32[8]{0:T(128)} %label_hbm.1, f32[3,64,1024]{2,1,0:T(8,128)} %bitcast.9, f32[64,100]{1,0:T(8,128)} %dual_hbm.1, f32[3,4,1024]{2,1,0:T(4,128)} %bitcast.15), custom_call_target="tpu_custom_call" | custom-call | bytes 2097152 | tf_op jit(solution)/shard_map/pick/pallas_call | solution.py:408
  5.3 4.0 %collective-permute-start.3 = (f32[24,1024]{1,0:T(8,128)S(1)}, f32[24,1024]{1,0:T(8,128)S(1)}, u32[]{:S(2)}, u32[]{:S(2)}) collective-permute-start(f32[24,1024]{1,0:T(8,128)S(1)} %get-tuple-element.34), channel_id=1, source_target_pairs={{0,32},{1,33},{2,34},{3,35},{4,36},{5,37},{6,38},{7,39},{8,40},{9,... | collective-permute-start | bytes 294920 | tf_op jit(solution)/shard_map/ppermute | solution.py:39
  9.3 0.7 %collective-permute-start.2 = (f32[24,1024]{1,0:T(8,128)S(1)}, f32[24,1024]{1,0:T(8,128)S(1)}, u32[]{:S(2)}, u32[]{:S(2)}) collective-permute-start(f32[24,1024]{1,0:T(8,128)S(1)} %get-tuple-element.34), channel_id=1, source_target_pairs={{0,48},{1,49},{2,50},{3,51},{4,52},{5,53},{6,54},{7,55},{8,56},{9,... | collective-permute-start | bytes 294920 | tf_op jit(solution)/shard_map/ppermute | solution.py:39
  10.0 0.3 collective-permute-start.1
  10.3 1.2 %collective-permute-done.5.s3_ref = f32[3,4,1024]{2,1,0:T(4,128)S(1)} collective-permute-done((f32[3,4,1024]{2,1,0:T(4,128)S(1)}, f32[3,4,1024]{2,1,0:T(4,128)S(1)}, u32[]{:S(2)}, u32[]{:S(2)}) %collective-permute-start.5) | collective-permute-done | bytes 49184 | tf_op jit(solution)/shard_map/ppermute | solution.py:39
  11.5 3.3 %spread.1 = (f32[3,32,16,8,128]{4,3,2,1,0:T(8,128)S(1)}, f32[3,32,16,8,128]{4,3,2,1,0:T(8,128)S(1)}, f32[3,32,16,8,128]{4,3,2,1,0:T(8,128)S(1)}) custom-call(f32[3,4,1024]{2,1,0:T(4,128)S(1)} %get-tuple-element.35.s0_ref, f32[3,4,1024]{2,1,0:T(4,128)S(1)} %collective-permute-done.s1_ref, f32[3,4,1024]{2,1,0:T(4,128)S(1)} %collective-permute-done.4.s2_ref, ...), custom_call_target="tpu_custom_call" | custom-call | bytes 12582912 | tf_op jit(solution)/shard_map/spread/pallas_call | solution.py:418
  15.3 8.7 %forward.1 = (f32[32,100]{1,0:T(8,128)S(1)}, f32[3,8,32,128]{3,2,1,0:T(8,128)S(1)}, f32[32,16,8,128]{3,2,1,0:T(8,128)S(1)}, f32[32,16,8,128]{3,2,1,0:T(8,128)S(1...) custom-call(f32[4,24,1024]{2,1,0:T(8,128)S(1)} %pad_maximum_fusion.x, ...), custom_call_target="tpu_custom_call" | custom-call | bytes 33554432 | tf_op jit(solution)/shard_map/forward/pallas_call | solution.py:433
  24.0 3.3 %collective-permute-start.8 = (f32[32,100]{1,0:T(8,128)S(1)}, f32[32,100]{1,0:T(8,128)S(1)}, u32[]{:S(2)}, u32[]{:S(2)}) collective-permute-start(f32[32,100]{1,0:T(8,128)S(1)} %get-tuple-element.44), channel_id=1, source_target_pairs={{0,32},{1,33},{2,34},{3,35},{4,36},{5,37},{6,38},{7,39},{8,40},{9,... | collective-permute-start | bytes 38408 | tf_op jit(solution)/shard_map/ppermute | solution.py:39
  27.3 0.7 %collective-permute-start.7 = (f32[32,100]{1,0:T(8,128)S(1)}, f32[32,100]{1,0:T(8,128)S(1)}, u32[]{:S(2)}, u32[]{:S(2)}) collective-permute-start(f32[32,100]{1,0:T(8,128)S(1)} %get-tuple-element.44), channel_id=1, source_target_pairs={{0,48},{1,49},{2,50},{3,51},{4,52},{5,53},{6,54},{7,55},{8,56},{9,... | collective-permute-start | bytes 38408 | tf_op jit(solution)/shard_map/ppermute | solution.py:39
  28.0 1.0 %back_a.1 = (f32[32,16,8,128]{3,2,1,0:T(8,128)S(1)}, f32[34,16,8,128]{3,2,1,0:T(8,128)S(1)}, f32[34,16,8,128]{3,2,1,0:T(8,128)S(1)}) custom-call(f32[34,16,8,128]{3,2,1,0:T(8,128)S(1)} %get-tuple-element.45.v2_ref, f32[32,16,8,128]{3,2,1,0:T(8,128)S(1)} %get-tuple-element.46.h1_ref, f32[32,16,8,128]{3,2,1,0:T(8,128)S(1)} %get-tuple-element.47.w1_ref, ...), custom_call_target="tpu_custom_call" | custom-call | bytes 5242880 | tf_op jit(solution)/shard_map/back_a/pallas_call | solution.py:428
  29.3 3.0 %collective-permute-done.7 = f32[32,100]{1,0:T(8,128)S(1)} collective-permute-done((f32[32,100]{1,0:T(8,128)S(1)}, f32[32,100]{1,0:T(8,128)S(1)}, u32[]{:S(2)}, u32[]{:S(2)}) %collective-permute-start.7) | collective-permute-done | bytes 12832 | tf_op jit(solution)/shard_map/ppermute | solution.py:39
  32.3 0.8 %collective-permute-start.9 = (f32[32,100]{1,0:T(8,128)S(1)}, f32[32,100]{1,0:T(8,128)S(1)}, u32[]{:S(2)}, u32[]{:S(2)}) collective-permute-start(f32[32,100]{1,0:T(8,128)S(1)} %add_add_fusion.1), channel_id=1, source_target_pairs={{0,4},{1,5},{2,6},{3,7},{4,0},{5,1},{6,2},{7,3},{8,12},{9,13},{10,... | collective-permute-start | bytes 38408 | tf_op jit(solution)/shard_map/ppermute | solution.py:39
  33.0 2.0 %back_b.1 = (f32[34,16,8,128]{3,2,1,0:T(8,128)S(1)}, f32[34,16,8,128]{3,2,1,0:T(8,128)S(1)}) custom-call(f32[34,16,8,128]{3,2,1,0:T(8,128)S(1)} %get-tuple-element.51.v1_ref, f32[32,16,8,128]{3,2,1,0:T(8,128)S(1)} %get-tuple-element.52.h0_ref, f32[32,16,8,128]{3,2,1,0:T(8,128)S(1)} %get-tuple-element.53.w0_ref, ...), custom_call_target="tpu_custom_call" | custom-call | bytes 6291456 | tf_op jit(solution)/shard_map/back_b/pallas_call | solution.py:428
  35.1 1.0 %collective-permute-done.9 = f32[32,100]{1,0:T(8,128)S(1)} collective-permute-done((f32[32,100]{1,0:T(8,128)S(1)}, f32[32,100]{1,0:T(8,128)S(1)}, u32[]{:S(2)}, u32[]{:S(2)}) %collective-permute-start.9) | collective-permute-done | bytes 12832 | tf_op jit(solution)/shard_map/ppermute | solution.py:39
  36.1 3.0 %collective-permute-start.12 = (f32[32,100]{1,0:T(8,128)S(1)}, f32[32,100]{1,0:T(8,128)S(1)}, u32[]{:S(2)}, u32[]{:S(2)}) collective-permute-start(f32[32,100]{1,0:T(8,128)S(1)} %add.30), channel_id=1, source_target_pairs={{0,2},{1,3},{2,0},{3,1},{4,6},{5,7},{6,4},{7,5},{8,10},{9,11},{10,... | collective-permute-start | bytes 38408 | tf_op jit(solution)/shard_map/ppermute | solution.py:39
  39.1 1.1 %collective-permute-start.11 = (f32[32,100]{1,0:T(8,128)S(1)}, f32[32,100]{1,0:T(8,128)S(1)}, u32[]{:S(2)}, u32[]{:S(2)}) collective-permute-start(f32[32,100]{1,0:T(8,128)S(1)} %add.30), channel_id=1, source_target_pairs={{0,3},{1,2},{2,1},{3,0},{4,7},{5,6},{6,5},{7,4},{8,11},{9,10},{10,... | collective-permute-start | bytes 38408 | tf_op jit(solution)/shard_map/ppermute | solution.py:39
  40.3 1.6 %back_c.1.g_ref = f32[3,32,16,8,128]{4,3,2,1,0:T(8,128)S(1)} custom-call(f32[34,16,8,128]{3,2,1,0:T(8,128)S(1)} %get-tuple-element.58.v0_ref, f32[34,16,8,128]{3,2,1,0:T(8,128)S(1)} %get-tuple-element.59.p0_ref, f32[3,8,32,128]{3,2,1,0:T(8,128)S(1)} %get-tuple-element.60.xt_ref, f32[3,32,16,8,128]{4,3,2,1,0:T(8,128)S(1)} %get-tuple-element.37.y_ref), custom_call_target="tpu_custom_call" | custom-call | bytes 5242880 | tf_op jit(solution)/shard_map/back_c/pallas_call | solution.py:428
  41.8 2.2 %collective-permute-done.11 = f32[32,100]{1,0:T(8,128)S(1)} collective-permute-done((f32[32,100]{1,0:T(8,128)S(1)}, f32[32,100]{1,0:T(8,128)S(1)}, u32[]{:S(2)}, u32[]{:S(2)}) %collective-permute-start.11) | collective-permute-done | bytes 12832 | tf_op jit(solution)/shard_map/ppermute | solution.py:39
  44.1 2.9 %weighted.1 = (f32[8,100]{1,0:T(8,128)}, f32[3,8,1024]{2,1,0:T(8,128)S(1)}, f32[3,8,1024]{2,1,0:T(8,128)S(1)}) custom-call(f32[32,100]{1,0:T(8,128)S(1)} %add_add_fusion.res_ref, f32[64,100]{1,0:T(8,128)S(1)} %get-tuple-element.40.dual_ref, f32[3,32,16,8,128]{4,3,2,1,0:T(8,128)S(1)} %back_c.1.g_ref), custom_call_target="tpu_custom_call" | custom-call | bytes 10485760 | tf_op jit(solution)/shard_map/weighted/pallas_call | solution.py:460
  46.9 1.3 %collective-permute-done.13 = f32[3,8,1024]{2,1,0:T(8,128)S(1)} collective-permute-done((f32[3,8,1024]{2,1,0:T(8,128)S(1)}, f32[3,8,1024]{2,1,0:T(8,128)S(1)}, u32[]{:S(2)}, u32[]{:S(2)}) %collective-permute-start.13) | collective-permute-done | bytes 98336 | tf_op jit(solution)/shard_map/ppermute | solution.py:39
  48.3 1.0 %collective-permute-start.14 = (f32[3,4,1024]{2,1,0:T(4,128)S(1)}, f32[3,4,1024]{2,1,0:T(4,128)S(1)}, u32[]{:S(2)}, u32[]{:S(2)}) collective-permute-start(f32[3,4,1024]{2,1,0:T(4,128)S(1)} %slice.9), channel_id=1, source_target_pairs={{0,64},{1,65},{2,66},{3,67},{4,68},{5,69},{6,70},{7,71},{8,72},{9,... | collective-permute-start | bytes 147464 | tf_op jit(solution)/shard_map/ppermute | solution.py:39
  49.3 4.7 %collective-permute-done.14 = f32[3,4,1024]{2,1,0:T(4,128)S(1)} collective-permute-done((f32[3,4,1024]{2,1,0:T(4,128)S(1)}, f32[3,4,1024]{2,1,0:T(4,128)S(1)}, u32[]{:S(2)}, u32[]{:S(2)}) %collective-permute-start.14) | collective-permute-done | bytes 49184 | tf_op jit(solution)/shard_map/ppermute | solution.py:39
  53.9 0.6 %fusion = f32[4,3,1024]{2,0,1:T(4,128)} fusion(f32[3,4,1024]{2,1,0:T(4,128)S(1)} %collective-permute-done.14, f32[3,8,1024]{2,1,0:T(8,128)S(1)} %add.34), kind=kLoop, calls=%fused_computation.2 | loop fusion | flops 12288 | bytes 147456 | tf_op jit(solution)/shard_map/transpose | solution.py:467
  (20 shorter events, 0.9 us)
Async XLA Ops:
  0.6 4.7 %collective-permute-start = (f32[3,4,1024]{2,1,0:T(4,128)}, f32[3,4,1024]{2,1,0:T(4,128)S(1)}, u32[]{:S(2)}, u32[]{:S(2)}) collective-permute-start(f32[3,4,1024]{2,1,0:T(4,128)} %bitcast.13), channel_id=1, source_target_pairs={{0,8},{1,9},{2,10},{3,11},{4,12},{5,13},{6,14},{7,15},{8,0},{9,1},... | collective-permute-start | bytes 147464 | tf_op jit(solution)/shard_map/ppermute | solution.py:39
  0.7 9.6 %collective-permute-start.4 = (f32[3,4,1024]{2,1,0:T(4,128)}, f32[3,4,1024]{2,1,0:T(4,128)S(1)}, u32[]{:S(2)}, u32[]{:S(2)}) collective-permute-start(f32[3,4,1024]{2,1,0:T(4,128)} %bitcast.14), channel_id=1, source_target_pairs={{0,64},{1,65},{2,66},{3,67},{4,68},{5,69},{6,70},{7,71},{8,72},{9,... | collective-permute-start | bytes 147464 | tf_op jit(solution)/shard_map/ppermute | solution.py:39
  5.3 9.5 %collective-permute-start.3 = (f32[24,1024]{1,0:T(8,128)S(1)}, f32[24,1024]{1,0:T(8,128)S(1)}, u32[]{:S(2)}, u32[]{:S(2)}) collective-permute-start(f32[24,1024]{1,0:T(8,128)S(1)} %get-tuple-element.34), channel_id=1, source_target_pairs={{0,32},{1,33},{2,34},{3,35},{4,36},{5,37},{6,38},{7,39},{8,40},{9,... | collective-permute-start | bytes 294920 | tf_op jit(solution)/shard_map/ppermute | solution.py:39
  9.3 5.8 %collective-permute-start.2 = (f32[24,1024]{1,0:T(8,128)S(1)}, f32[24,1024]{1,0:T(8,128)S(1)}, u32[]{:S(2)}, u32[]{:S(2)}) collective-permute-start(f32[24,1024]{1,0:T(8,128)S(1)} %get-tuple-element.34), channel_id=1, source_target_pairs={{0,48},{1,49},{2,50},{3,51},{4,52},{5,53},{6,54},{7,55},{8,56},{9,... | collective-permute-start | bytes 294920 | tf_op jit(solution)/shard_map/ppermute | solution.py:39
  10.0 5.3 %collective-permute-start.1 = (f32[24,1024]{1,0:T(8,128)S(1)}, f32[24,1024]{1,0:T(8,128)S(1)}, u32[]{:S(2)}, u32[]{:S(2)}) collective-permute-start(f32[24,1024]{1,0:T(8,128)S(1)} %get-tuple-element.34), channel_id=1, source_target_pairs={{0,16},{1,17},{2,18},{3,19},{4,20},{5,21},{6,22},{7,23},{8,24},{9,... | collective-permute-start | bytes 294920 | tf_op jit(solution)/shard_map/ppermute | solution.py:39
  10.3 1.2 %collective-permute-start.5 = (f32[3,4,1024]{2,1,0:T(4,128)S(1)}, f32[3,4,1024]{2,1,0:T(4,128)S(1)}, u32[]{:S(2)}, u32[]{:S(2)}) collective-permute-start(f32[3,4,1024]{2,1,0:T(4,128)S(1)} %collective-permute-done.4.s2_ref), channel_id=1, source_target_pairs={{0,8},{1,9},{2,10},{3,11},{4,12},{5,13},{6,14},{7,15},{8,0},{9,1},... | collective-permute-start | bytes 147464 | tf_op jit(solution)/shard_map/ppermute | solution.py:39
  24.0 5.3 %collective-permute-start.8 = (f32[32,100]{1,0:T(8,128)S(1)}, f32[32,100]{1,0:T(8,128)S(1)}, u32[]{:S(2)}, u32[]{:S(2)}) collective-permute-start(f32[32,100]{1,0:T(8,128)S(1)} %get-tuple-element.44), channel_id=1, source_target_pairs={{0,32},{1,33},{2,34},{3,35},{4,36},{5,37},{6,38},{7,39},{8,40},{9,... | collective-permute-start | bytes 38408 | tf_op jit(solution)/shard_map/ppermute | solution.py:39
  27.3 4.9 %collective-permute-start.7 = (f32[32,100]{1,0:T(8,128)S(1)}, f32[32,100]{1,0:T(8,128)S(1)}, u32[]{:S(2)}, u32[]{:S(2)}) collective-permute-start(f32[32,100]{1,0:T(8,128)S(1)} %get-tuple-element.44), channel_id=1, source_target_pairs={{0,48},{1,49},{2,50},{3,51},{4,52},{5,53},{6,54},{7,55},{8,56},{9,... | collective-permute-start | bytes 38408 | tf_op jit(solution)/shard_map/ppermute | solution.py:39
  28.0 4.2 %collective-permute-start.6 = (f32[32,100]{1,0:T(8,128)S(1)}, f32[32,100]{1,0:T(8,128)S(1)}, u32[]{:S(2)}, u32[]{:S(2)}) collective-permute-start(f32[32,100]{1,0:T(8,128)S(1)} %get-tuple-element.44), channel_id=1, source_target_pairs={{0,16},{1,17},{2,18},{3,19},{4,20},{5,21},{6,22},{7,23},{8,24},{9,... | collective-permute-start | bytes 38408 | tf_op jit(solution)/shard_map/ppermute | solution.py:39
  32.3 3.8 %collective-permute-start.9 = (f32[32,100]{1,0:T(8,128)S(1)}, f32[32,100]{1,0:T(8,128)S(1)}, u32[]{:S(2)}, u32[]{:S(2)}) collective-permute-start(f32[32,100]{1,0:T(8,128)S(1)} %add_add_fusion.1), channel_id=1, source_target_pairs={{0,4},{1,5},{2,6},{3,7},{4,0},{5,1},{6,2},{7,3},{8,12},{9,13},{10,... | collective-permute-start | bytes 38408 | tf_op jit(solution)/shard_map/ppermute | solution.py:39
  36.1 5.7 %collective-permute-start.12 = (f32[32,100]{1,0:T(8,128)S(1)}, f32[32,100]{1,0:T(8,128)S(1)}, u32[]{:S(2)}, u32[]{:S(2)}) collective-permute-start(f32[32,100]{1,0:T(8,128)S(1)} %add.30), channel_id=1, source_target_pairs={{0,2},{1,3},{2,0},{3,1},{4,6},{5,7},{6,4},{7,5},{8,10},{9,11},{10,... | collective-permute-start | bytes 38408 | tf_op jit(solution)/shard_map/ppermute | solution.py:39
  39.1 4.9 %collective-permute-start.11 = (f32[32,100]{1,0:T(8,128)S(1)}, f32[32,100]{1,0:T(8,128)S(1)}, u32[]{:S(2)}, u32[]{:S(2)}) collective-permute-start(f32[32,100]{1,0:T(8,128)S(1)} %add.30), channel_id=1, source_target_pairs={{0,3},{1,2},{2,1},{3,0},{4,7},{5,6},{6,5},{7,4},{8,11},{9,10},{10,... | collective-permute-start | bytes 38408 | tf_op jit(solution)/shard_map/ppermute | solution.py:39
  40.2 3.8 %collective-permute-start.10 = (f32[32,100]{1,0:T(8,128)S(1)}, f32[32,100]{1,0:T(8,128)S(1)}, u32[]{:S(2)}, u32[]{:S(2)}) collective-permute-start(f32[32,100]{1,0:T(8,128)S(1)} %add.30), channel_id=1, source_target_pairs={{0,1},{1,0},{2,3},{3,2},{4,5},{5,4},{6,7},{7,6},{8,9},{9,8},{10,11... | collective-permute-start | bytes 38408 | tf_op jit(solution)/shard_map/ppermute | solution.py:39
  46.9 1.3 %collective-permute-start.13 = (f32[3,8,1024]{2,1,0:T(8,128)S(1)}, f32[3,8,1024]{2,1,0:T(8,128)S(1)}, u32[]{:S(2)}, u32[]{:S(2)}) collective-permute-start(f32[3,8,1024]{2,1,0:T(8,128)S(1)} %get-tuple-element.63), channel_id=1, source_target_pairs={{0,8},{1,9},{2,10},{3,11},{4,12},{5,13},{6,14},{7,15},{8,0},{9,1},... | collective-permute-start | bytes 294920 | tf_op jit(solution)/shard_map/ppermute | solution.py:39
  48.3 5.7 %collective-permute-start.14 = (f32[3,4,1024]{2,1,0:T(4,128)S(1)}, f32[3,4,1024]{2,1,0:T(4,128)S(1)}, u32[]{:S(2)}, u32[]{:S(2)}) collective-permute-start(f32[3,4,1024]{2,1,0:T(4,128)S(1)} %slice.9), channel_id=1, source_target_pairs={{0,64},{1,65},{2,66},{3,67},{4,68},{5,69},{6,70},{7,71},{8,72},{9,... | collective-permute-start | bytes 147464 | tf_op jit(solution)/shard_map/ppermute | solution.py:39
